TPU v7x, 128 devices: a whole 4x4x4 slice. The times are simulated.
128 devices in a mesh: dp: 8 (over z_hi, x), seq: 8 (over z_lo, y), mp: 2 (over core).
Axes of the slice: x: 4, y: 4, z: 4 (z_hi: 2, z_lo: 2; z = z_hi * 2 + z_lo), core: 2. Of those that a mesh axis runs over, the one named last changes fastest.
Arguments:
- queries: bfloat16 [8, 4096, 4096], P('dp', 'seq', 'mp'), may hold values from -140 to 140
- features: bfloat16 [8, 1024, 7680], P(None, ('seq', 'dp')), may hold values from -12 to 12
- w_key: bfloat16 [7680, 512], P(None, 'mp'), may hold values from -0.0625 to 0.0625
- w_value: bfloat16 [7680, 512], P(None, 'mp'), may hold values from -0.0625 to 0.0625
- key_gain: float32 [128], replicated, may hold values from 0.25 to 1.75
- out_grad: bfloat16 [8, 4096, 4096], P('dp', 'seq', 'mp'), may hold values from -6 to 6
- tile_counts: int32 [8], P('dp'), may hold values from 1 to 4, as said below
- text_start: int32 [8], P('dp'), may hold values from 0 to 2048, as said below
Outputs:
- attended: bfloat16 [8, 4096, 4096], P('dp', 'seq', 'mp')
- query_grad: bfloat16 [8, 4096, 4096], P('dp', 'seq', 'mp')
- key_weight_grad: float32 [7680, 512], P(('dp', 'seq'), 'mp')
- value_weight_grad: float32 [7680, 512], P(('dp', 'seq'), 'mp')
Inputs may be any that keep to these rules, and one draw needn't show every extreme that they name: Image positions of row b from tile_counts[b] * 256 on are padding that no query sees. Text positions of row b below text_start[b] come before the row's image: they attend to nothing, their output and gradients are zero.
All inputs are finite; a program needn't handle non-finite values.
Results may differ from a plain program's by a relative error of at most 0.035.
The roundings to bfloat16 on the way count: a program that leaves them out, or rounds other values in their place, can miss the bound.
Values may be sent and summed in bfloat16 or wider, within the bound.
No kernel may reach another device: no remote copies, remote signals or barrier semaphores. Data moves between devices by JAX's collectives and lax.ppermute only.
A program may use at most 128 MiB of HBM per device.

v0:
```python
import jax
import jax.numpy as jnp
from jax import lax
from jax.sharding import PartitionSpec as P

FEAT = 7680
HEAD_DIM = 128
TILES = 4


EPSILON = 1e-05


def normalize_keys(key_pre, key_gain):
    head_rows = key_pre.reshape(key_pre.shape[0], -1, HEAD_DIM)
    factor = lax.rsqrt(jnp.mean(head_rows * head_rows, axis=-1, keepdims=True) + EPSILON)
    return (head_rows, factor, head_rows * factor * key_gain)


def normalize_back(head_rows, factor, key_gain, key_grad):
    gained = key_gain * key_grad
    inner_mean = jnp.mean(head_rows * gained, axis=-1, keepdims=True)
    return factor * gained - factor * factor * factor * head_rows * inner_mean


def group_pass(q_group, k_group, v_group, d_group, key_valid, live_rows):
    score_scale = HEAD_DIM ** (-0.5)
    scores = jnp.dot(q_group, k_group.T, preferred_element_type=jnp.float32) * score_scale
    scores = jnp.where(key_valid[None, :], scores, -jnp.inf)
    row_max = jnp.max(scores, axis=1, keepdims=True)
    powers = jnp.exp(scores - row_max)
    probabilities = powers / jnp.sum(powers, axis=1, keepdims=True)
    prob_rounded = probabilities.astype(jnp.bfloat16)
    output_part = (
        jnp.dot(prob_rounded, v_group, preferred_element_type=jnp.float32) * live_rows[:, None]
    ).astype(jnp.bfloat16)
    grad_live = d_group * live_rows[:, None].astype(d_group.dtype)
    prob_grad = jnp.dot(grad_live, v_group.T, preferred_element_type=jnp.float32)
    row_delta = jnp.sum(probabilities * prob_grad, axis=1, keepdims=True)
    score_grad = (probabilities * (prob_grad - row_delta)).astype(jnp.bfloat16)
    query_part = (
        jnp.dot(score_grad, k_group, preferred_element_type=jnp.float32) * score_scale
    ).astype(jnp.bfloat16)
    key_part = jnp.dot(score_grad.T, q_group, preferred_element_type=jnp.float32) * score_scale
    value_part = jnp.dot(prob_rounded.T, grad_live, preferred_element_type=jnp.float32)
    return (output_part, query_part, key_part, value_part)


def on_device(queries, features, w_key, w_value, key_gain, out_grad, tile_counts, text_start):
    seq_index = lax.axis_index("seq")
    text_dev = queries.shape[1]
    kv_dim = w_key.shape[1]
    groups = kv_dim // HEAD_DIM
    group_size = queries.shape[2] // kv_dim
    arrived = lax.all_to_all(features, "dp", split_axis=0, concat_axis=1, tiled=True)
    tokens_mat = arrived.reshape(-1, FEAT)
    key_pre = jnp.dot(tokens_mat, w_key, preferred_element_type=jnp.float32)
    head_rows, factor, normed = normalize_keys(key_pre, key_gain)
    keys_here = normed.astype(jnp.bfloat16).reshape(-1, kv_dim)
    values_here = jnp.dot(tokens_mat, w_value, preferred_element_type=jnp.float32).astype(
        jnp.bfloat16
    )
    keys_all, values_all = (
        lax.all_gather(keys_here, "seq", axis=0, tiled=True),
        lax.all_gather(values_here, "seq", axis=0, tiled=True),
    )
    img_len = keys_all.shape[0]
    key_valid = jnp.arange(img_len, dtype=jnp.int32) < tile_counts[0] * (img_len // TILES)
    positions = seq_index * text_dev + jnp.arange(text_dev, dtype=jnp.int32)
    live_mask = (positions >= text_start[0]).astype(jnp.float32)
    block_len = min(256, text_dev)
    block_count = text_dev // block_len
    live_rows = jnp.repeat(live_mask, group_size).reshape(block_count, block_len * group_size)
    q_groups = queries[0].reshape(block_count, block_len, groups, group_size, HEAD_DIM)
    d_groups = out_grad[0].reshape(block_count, block_len, groups, group_size, HEAD_DIM)
    keys_split = keys_all.reshape(img_len, groups, HEAD_DIM)
    values_split = values_all.reshape(img_len, groups, HEAD_DIM)
    attended_parts = []
    query_parts = []
    key_parts = []
    value_parts = []
    for member in range(groups):
        k_group = keys_split[:, member]
        v_group = values_split[:, member]
        q_blocks = q_groups[:, :, member].reshape(block_count, block_len * group_size, HEAD_DIM)
        d_blocks = d_groups[:, :, member].reshape(block_count, block_len * group_size, HEAD_DIM)

        def block_step(running, block_item):
            output_part, query_part, key_part, value_part = group_pass(
                block_item[0], k_group, v_group, block_item[1], key_valid, block_item[2]
            )
            return ((running[0] + key_part, running[1] + value_part), (output_part, query_part))

        zero_grad = jnp.zeros((img_len, HEAD_DIM), jnp.float32)
        sums, block_outs = lax.scan(
            block_step, (zero_grad, zero_grad), (q_blocks, d_blocks, live_rows)
        )
        key_share, value_share = (
            lax.psum_scatter(
                sums[0].astype(jnp.bfloat16), "seq", scatter_dimension=0, tiled=True
            ).astype(jnp.float32),
            lax.psum_scatter(
                sums[1].astype(jnp.bfloat16), "seq", scatter_dimension=0, tiled=True
            ).astype(jnp.float32),
        )
        attended_parts.append(block_outs[0].reshape(block_count, block_len, group_size * HEAD_DIM))
        query_parts.append(block_outs[1].reshape(block_count, block_len, group_size * HEAD_DIM))
        key_parts.append(key_share)
        value_parts.append(value_share)
    attended = jnp.stack(attended_parts, axis=2).reshape(1, text_dev, kv_dim * group_size)
    query_grad = jnp.stack(query_parts, axis=2).reshape(1, text_dev, kv_dim * group_size)
    key_grad = jnp.stack(key_parts, axis=1)
    value_grad = jnp.stack(value_parts, axis=1).reshape(-1, kv_dim)
    pre_grad = (
        normalize_back(head_rows, factor, key_gain, key_grad)
        .reshape(-1, kv_dim)
        .astype(jnp.bfloat16)
    )
    grads_rounded = jnp.concatenate([pre_grad, value_grad.astype(jnp.bfloat16)], axis=1)
    summed = lax.psum_scatter(
        lax.dot_general(
            tokens_mat, grads_rounded, (((0,), (0,)), ((), ())), preferred_element_type=jnp.float32
        ),
        ("dp", "seq"),
        scatter_dimension=0,
        tiled=True,
    )
    return (attended, query_grad, summed[:, :kv_dim], summed[:, kv_dim:])


def solution(mesh):
    placed = (
        P("dp", "seq", "mp"),
        P(None, ("seq", "dp"), None),
        P(None, "mp"),
        P(None, "mp"),
        P(),
        P("dp", "seq", "mp"),
        P("dp"),
        P("dp"),
    )
    return jax.shard_map(
        on_device,
        mesh=mesh,
        in_specs=placed,
        out_specs=(
            P("dp", "seq", "mp"),
            P("dp", "seq", "mp"),
            P(("dp", "seq"), "mp"),
            P(("dp", "seq"), "mp"),
        ),
        check_vma=False,
    )
```

profile of v0, /device:TPU:0, one launch (start us, length us, event | category | flops | bytes accessed | tf_op | source)
XLA Modules:
  0.0 731.6 jit_solution(16033248463245938596)
XLA Ops:
  7.2 7.7 %all-to-all-start = ((bf16[8,16,7680]{2,1,0:T(8,128)(2,1)}), bf16[8,16,7680]{2,1,0:T(8,128)(2,1)}, u32[]{:S(2)}, u32[]{:S(2)}) async-start(bf16[8,16,7680]{2,1,0:T(8,128)(2,1)} %param.13), calls=%async_computation | async-start | bytes 3932160 | tf_op jit(solution)/shard_map/all_to_all | solution.py:55
  16.5 3.5 copy.84
  20.1 3.5 copy.85
  23.6 6.2 copy.65
  29.9 3.9 slice_bitcast_fusion.2
  33.7 8.3 %all-to-all-done = bf16[8,16,7680]{2,1,0:T(8,128)(2,1)} async-done(((bf16[8,16,7680]{2,1,0:T(8,128)(2,1)}), bf16[8,16,7680]{2,1,0:T(8,128)(2,1)}, u32[]{:S(2)}, u32[]{:S(2)}) %all-to-all-start) | async-done | bytes 1966112 | tf_op jit(solution)/shard_map/all_to_all | solution.py:55
  42.0 3.4 convolution_convert_fusion
  45.4 29.0 %all_gather.7 = bf16[1024,256]{1,0:T(8,128)(2,1)S(1)} all-gather(bf16[128,256]{1,0:T(8,128)(2,1)S(1)} %convolution_convert_fusion), channel_id=1, replica_groups=mesh['dp'=8,'seq'=8,'mp'=2] {'seq'}, dimensions={0}, use_global_device_ids=true | all-gather | bytes 589824 | tf_op jit(solution)/shard_map/all_gather | solution.py:65
  75.3 3.9 multiply_reduce_fusion.3
  79.9 25.7 %all_gather.6 = bf16[1024,256]{0,1:T(8,128)(2,1)S(1)} all-gather(bf16[128,256]{0,1:T(8,128)(2,1)S(1)} %bitcast.185), channel_id=1, replica_groups=mesh['dp'=8,'seq'=8,'mp'=2] {'seq'}, dimensions={0}, use_global_device_ids=true | all-gather | bytes 589824 | tf_op jit(solution)/shard_map/all_gather | solution.py:64
  109.6 49.1 %while.34 = (s32[]{:T(128)}, f32[1024,128]{1,0:T(8,128)S(1)}, f32[1024,128]{1,0:T(8,128)}, bf16[2,2048,128]{2,1,0:T(8,128)(2,1)}, bf16[2,2048,128]{2,1,0:T(8,128...) while((s32[]{:T(128)}, f32[1024,128]{1,0:T(8,128)S(1)}, ...), condition=%wide.region_5.6_spmd.clone, body=%wide.region_1.5_spmd.clone.sunk | while | flops 3286365184 | bytes 112356760 | solution.py:95
  111.3 2.5 fusion.127
  113.9 2.4 fusion.129
  116.3 2.7 fusion.130
  119.0 2.8 multiply_reduce_fusion.6
  121.8 3.3 multiply_convert_fusion.5
  126.6 1.6 fusion.131
  130.4 2.5 fusion.127
  133.0 2.4 fusion.129
  135.4 2.7 fusion.130
  138.1 2.8 multiply_reduce_fusion.6
  140.9 3.3 multiply_convert_fusion.5
  145.6 1.6 fusion.131
  163.4 36.4 %while.35 = (s32[]{:T(128)}, f32[1024,128]{1,0:T(8,128)S(1)}, f32[1024,128]{1,0:T(8,128)}, bf16[2,2048,128]{2,1,0:T(8,128)(2,1)}, bf16[2,2048,128]{2,1,0:T(8,128...) while((s32[]{:T(128)}, f32[1024,128]{1,0:T(8,128)S(1)}, ...), condition=%wide.region_10.11_spmd.clone, body=%wide.region_6.10_spmd.clone.sunk | while | flops 3286365184 | bytes 103968096 | solution.py:95
  164.8 2.5 fusion.142
  167.3 2.4 fusion.144
  169.7 2.7 fusion.145
  172.4 2.8 multiply_reduce_fusion.7
  175.2 3.4 multiply_convert_fusion.6
  180.0 1.5 fusion.146
  182.9 2.5 fusion.142
  185.4 2.4 fusion.144
  187.8 2.7 fusion.145
  190.5 2.8 multiply_reduce_fusion.7
  193.3 3.4 multiply_convert_fusion.6
  203.9 30.5 %reduce-scatter.20.cloned.1.call-done = bf16[128,128]{1,0:T(8,128)(2,1)} async-done(((bf16[1024,128]{1,0:T(8,128)(2,1)}), bf16[128,128]{1,0:T(8,128)(2,1)}) %reduce-scatter.20.cloned.1.call-update) | async-done | bytes 32784
  235.2 37.5 %reduce-scatter.18.cloned.1.call-done = bf16[128,128]{1,0:T(8,128)(2,1)} async-done(((bf16[1024,128]{1,0:T(8,128)(2,1)}), bf16[128,128]{1,0:T(8,128)(2,1)}) %reduce-scatter.18.cloned.1.call-update) | async-done | bytes 32784
  273.8 37.8 %reduce-scatter.22.cloned.1.call-done = bf16[128,128]{1,0:T(8,128)(2,1)} async-done(((bf16[1024,128]{1,0:T(8,128)(2,1)}), bf16[128,128]{1,0:T(8,128)(2,1)}) %reduce-scatter.22.cloned.1.call-update) | async-done | bytes 32784
  312.5 9.2 %convolution_bitcast_fusion = f32[7680,512]{0,1:T(8,128)} fusion(bf16[128,7680]{1,0:T(8,128)(2,1)} %bitcast.1, bf16[128,256]{0,1:T(8,128)(2,1)S(1)} %bitcast.183, bf16[128,256]{0,1:T(8,128)(2,1)S(1)} %bitcast.184), kind=kOutput, calls=%fused_computation.74 | convolution fusion | flops 1006895104 | bytes 17825792 | tf_op jit(solution)/shard_map/dot_general | solution.py:121
  321.7 15.6 %copy.74 = f32[7680,512]{1,0:T(8,128)} copy(f32[7680,512]{0,1:T(8,128)} %convolution_bitcast_fusion) | data formatting | bytes 31457280
  337.9 7.0 stack_reshape.18
  344.8 6.7 pad_maximum_fusion.1
  351.5 4.5 reshape.91
  356.5 6.9 stack_reshape.16
  363.3 6.7 pad_maximum_fusion
  370.0 4.5 reshape.90
  374.5 348.7 %reduce-scatter.24.cloned.1.call-done = f32[120,512]{1,0:T(8,128)} async-done(((f32[7680,512]{1,0:T(8,128)}), f32[120,512]{1,0:T(8,128)}) %reduce-scatter.24.cloned.1.call-update) | async-done | bytes 245776
  723.2 1.7 fusion.69
  (145 shorter events, 32.6 us)
Async XLA Ops:
  7.2 34.8 %all-to-all-start = ((bf16[8,16,7680]{2,1,0:T(8,128)(2,1)}), bf16[8,16,7680]{2,1,0:T(8,128)(2,1)}, u32[]{:S(2)}, u32[]{:S(2)}) async-start(bf16[8,16,7680]{2,1,0:T(8,128)(2,1)} %param.13), calls=%async_computation | async-start | bytes 3932160 | tf_op jit(solution)/shard_map/all_to_all | solution.py:55
  14.9 188.1 %reduce-scatter.16.cloned.1.call-start = ((), (), s32[]{:S(2)}) async-start(), calls=%async_computation.6 | async-start | bytes 294912
  33.7 46.0 %copy-start.21 = (f32[128]{0:T(128)S(1)}, f32[128]{0:T(128)}, u32[]{:S(2)}) copy-start(f32[128]{0:T(128)} %param.16) | copy-start | bytes 1540
  79.2 27.2 %copy-start.8 = (f32[128,2,128]{0,2,1:T(8,128)}, f32[128,2,128]{0,2,1:T(8,128)S(1)}, u32[]{:S(2)}) copy-start(f32[128,2,128]{0,2,1:T(8,128)S(1)} %get-tuple-element.331) | copy-start | bytes 393220
  79.8 26.6 %copy-start.19 = (f32[128,2]{0,1:T(2,128)}, f32[128,2]{0,1:T(2,128)S(1)}, u32[]{:S(2)}) copy-start(f32[128,2]{0,1:T(2,128)S(1)} %get-tuple-element.329) | copy-start | bytes 3076
  109.6 52.3 %copy-start.10 = (bf16[1024,128]{0,1:T(8,128)(2,1)S(1)}, bf16[1024,128]{0,1:T(8,128)(2,1)}, u32[]{:S(2)}) copy-start(bf16[1024,128]{0,1:T(8,128)(2,1)} %get-tuple-element.325) | copy-start | bytes 786436
  109.6 53.8 %copy-start = (bf16[2,2048,128]{2,1,0:T(8,128)(2,1)S(1)}, bf16[2,2048,128]{2,1,0:T(8,128)(2,1)}, u32[]{:S(2)}) copy-start(bf16[2,2048,128]{2,1,0:T(8,128)(2,1)} %get-tuple-element.491) | copy-start | bytes 3145732
  110.1 3.8 copy-start.12
  110.1 3.8 copy-start.13
  113.9 2.4 copy-start.4
  113.9 2.4 copy-start.18
  116.3 2.7 copy-start.14
  119.0 2.8 copy-start.5
  121.8 4.8 copy-start.6
  128.1 1.0 copy-start.7
  129.1 3.8 copy-start.12
  129.1 3.8 copy-start.13
  132.9 2.4 copy-start.4
  133.0 2.4 copy-start.18
  135.4 2.7 copy-start.14
  138.0 2.8 copy-start.5
  140.9 4.8 copy-start.6
  147.2 1.0 copy-start.7
  159.8 74.5 %reduce-scatter.20.cloned.1.call-start = ((), (), s32[]{:S(2)}) async-start(), calls=%async_computation.8 | async-start | bytes 294912
  162.1 110.6 %reduce-scatter.18.cloned.1.call-start = ((), (), s32[]{:S(2)}) async-start(), calls=%async_computation.7 | async-start | bytes 294912
  163.4 110.2 %copy-start.9 = (f32[128,2,128]{0,2,1:T(8,128)S(1)}, f32[128,2,128]{0,2,1:T(8,128)}, u32[]{:S(2)}) copy-start(f32[128,2,128]{0,2,1:T(8,128)} %copy-done.8) | copy-start | bytes 393220
  163.4 110.2 %copy-start.22 = (f32[128]{0:T(128)S(1)}, f32[128]{0:T(128)}, u32[]{:S(2)}) copy-start(f32[128]{0:T(128)} %param.16) | copy-start | bytes 1540
  163.4 110.3 %copy-start.20 = (f32[128,2]{0,1:T(2,128)S(1)}, f32[128,2]{0,1:T(2,128)}, u32[]{:S(2)}) copy-start(f32[128,2]{0,1:T(2,128)} %copy-done.19) | copy-start | bytes 3076
  163.4 110.3 %copy-start.23 = (f32[128,2]{0,1:T(2,128)S(1)}, f32[128,2]{0,1:T(2,128)}, u32[]{:S(2)}) copy-start(f32[128,2]{0,1:T(2,128)} %get-tuple-element.328) | copy-start | bytes 3076
  163.5 3.8 copy-start.11
  163.5 3.8 copy-start.15
  167.3 2.4 copy-start.1
  167.3 2.4 copy-start.17
  169.7 2.7 copy-start.16
  172.4 2.8 copy-start.2
  181.6 3.8 copy-start.11
  181.6 3.8 copy-start.15
  185.4 2.4 copy-start.1
  185.4 2.4 copy-start.17
  187.8 2.7 copy-start.16
  190.5 2.8 copy-start.2
  200.8 110.8 %reduce-scatter.22.cloned.1.call-start = ((), (), s32[]{:S(2)}) async-start(), calls=%async_computation.9 | async-start | bytes 294912
  202.9 520.2 %reduce-scatter.24.cloned.1.call-start = ((), (), s32[]{:S(2)}) async-start(), calls=%async_computation.10 | async-start | bytes 15974400
  337.9 18.1 %copy-start.3 = (bf16[2,2048,128]{2,1,0:T(8,128)(2,1)S(1)}, bf16[2,2048,128]{2,1,0:T(8,128)(2,1)}, u32[]{:S(2)}) copy-start(bf16[2,2048,128]{2,1,0:T(8,128)(2,1)} %get-tuple-element.125) | copy-start | bytes 3145732
Sparse Core Ops, SparseCore 0:
  159.9 35.8 reduce-scatter.15
  198.3 35.9 reduce-scatter.19
  236.7 35.9 reduce-scatter.17
  275.6 35.9 reduce-scatter.21
  337.5 385.6 reduce-scatter.23
where the time goes:
time: 737 us; the launch traced here: 732 us
  waiting for transfers between devices  463 us (63%)
  local copies, waits for them, and re-layouts  76.4 us (10%)
  matrix products  64.6 us (9%)
  blocking collectives  54.8 us (7%)
  other arithmetic  37.7 us (5%)
  between operations  15.6 us (2%)
  loops' own time  11.8 us (2%)
  starting transfers between devices  7.91 us (1%)
    unnamed x10, waiting for transfers between devices  455 us
    unnamed x33, local copies, waits for them, and re-layouts  29.9 us
    all_gather x1, blocking collectives, on_device(): lax.all_gather(values_here, 'seq', axis=0, tiled=True)  29 us
    all_gather x1, blocking collectives, on_device(): lax.all_gather(keys_here, 'seq', axis=0, tiled=True)  25.7 us
  transfers between devices with their start and end apart: 6, of which 5 were waited for; matrix products, arithmetic and copies ran while one was open for 14% of the time, Pallas kernels for 0%

commit v1 on v0

v1 whole, which is shorter than its diff:
```python
import functools

import jax
import jax.numpy as jnp
from jax import lax
from jax.experimental import pallas as pl
from jax.experimental.pallas import tpu as pltpu
from jax.sharding import PartitionSpec as P

HEAD_DIM = 128
TILES = 4
EPSILON = 1e-05
SCALE = HEAD_DIM**-0.5
EXP2_SCALE = SCALE * 1.4426950408889634
BF16 = jnp.bfloat16
F32 = jnp.float32
LANES = 128
VMEM_LIMIT = 48 * 2**20

NN = (((1,), (0,)), ((), ()))
NT = (((1,), (1,)), ((), ()))


def whole(shape):
    return pl.BlockSpec(shape, lambda *_: (0,) * len(shape))


def params(axes):
    return pltpu.CompilerParams(
        vmem_limit_bytes=VMEM_LIMIT, dimension_semantics=("arbitrary",) * axes
    )


def project_kernel(f_ref, wk_ref, wv_ref, gain_ref, *refs, windows, per_step, groups, copies):
    send_refs, (pre_ref, win_ref, total) = refs[:groups], refs[groups:]
    step, steps = pl.program_id(0), pl.num_programs(0)
    depth = wk_ref.shape[0]
    kv_dim = wk_ref.shape[1]
    width = win_ref.shape[2]
    part = f_ref[:, pl.ds(pl.multiple_of(step * depth, LANES), depth)]

    @pl.when(step == 0)
    def _():
        total[...] = jnp.zeros_like(total)

    total[:, :kv_dim] += jnp.dot(part, wk_ref[...], preferred_element_type=F32)
    total[:, kv_dim:] += jnp.dot(part, wv_ref[...], preferred_element_type=F32)

    @pl.when(step * per_step < windows)
    def _():
        for inner in range(per_step):
            at = step * per_step + inner
            tiles_all = f_ref.shape[1] // LANES
            tile = (at * tiles_all) // windows
            win_ref[inner] = f_ref[:, pl.ds(pl.multiple_of(tile * LANES, LANES), width)]

    @pl.when(step == steps - 1)
    def _():
        pre_ref[...] = total[:, :kv_dim]
        for group in range(groups):
            cols = slice(group * HEAD_DIM, (group + 1) * HEAD_DIM)
            head = total[:, cols]
            factor = lax.rsqrt(jnp.mean(head * head, axis=-1, keepdims=True) + EPSILON)
            key = (head * factor * gain_ref[...]).astype(BF16)
            start = kv_dim + group * HEAD_DIM
            value = total[:, start : start + HEAD_DIM].astype(BF16)
            for copy in range(copies):
                send_refs[group][copy, :, :HEAD_DIM] = key
                send_refs[group][copy, :, HEAD_DIM:] = value


def project(feats, w_key, w_value, gain, windows, copies):
    tokens, feat = feats.shape
    kv_dim = w_key.shape[1]
    groups = kv_dim // HEAD_DIM
    per_step = 2
    steps = windows // per_step + 1
    depth = feat // steps
    width = -(-(feat // windows) // LANES) * LANES
    last = windows // per_step - 1
    sends = [jax.ShapeDtypeStruct((copies, tokens, 2 * HEAD_DIM), BF16)] * groups
    return pl.pallas_call(
        functools.partial(
            project_kernel, windows=windows, per_step=per_step, groups=groups, copies=copies
        ),
        grid=(steps,),
        in_specs=[
            whole((tokens, feat)),
            pl.BlockSpec((depth, kv_dim), lambda k: (k, 0)),
            pl.BlockSpec((depth, kv_dim), lambda k: (k, 0)),
            whole((1, HEAD_DIM)),
        ],
        out_specs=[whole(s.shape) for s in sends]
        + [
            whole((tokens, kv_dim)),
            pl.BlockSpec((per_step, tokens, width), lambda k: (jnp.minimum(k, last), 0, 0)),
        ],
        out_shape=sends
        + [
            jax.ShapeDtypeStruct((tokens, kv_dim), F32),
            jax.ShapeDtypeStruct((windows, tokens, width), BF16),
        ],
        scratch_shapes=[pltpu.VMEM((tokens, 2 * kv_dim), F32)],
        compiler_params=params(1),
        cost_estimate=pl.CostEstimate(
            flops=4 * tokens * feat * kv_dim,
            bytes_accessed=4 * feat * kv_dim + 4 * tokens * feat,
            transcendentals=0,
        ),
        name="project",
    )(feats, w_key, w_value, gain)


def attend_kernel(ctl_ref, q_ref, d_ref, kv_ref, *refs, heads):
    att_ref, dq_ref, dkv_ref, kt_ref, vt_ref, dk_sum, dv_sum = refs[-7:]
    step, steps = pl.program_id(0), pl.num_programs(0)
    rows = q_ref.shape[0]
    img = kv_ref.shape[0]

    @pl.when(step == 0)
    def _():
        dk_sum[...] = jnp.zeros_like(dk_sum)
        dv_sum[...] = jnp.zeros_like(dv_sum)
        kt_ref[...] = kv_ref[:, :HEAD_DIM].T
        vt_ref[...] = kv_ref[:, HEAD_DIM:].T

    def run(length):
        key, value = kv_ref[:length, :HEAD_DIM], kv_ref[:length, HEAD_DIM:]
        key_t, value_t = kt_ref[:, :length], vt_ref[:, :length]
        position = ctl_ref[1] + lax.broadcasted_iota(jnp.int32, (rows, HEAD_DIM), 0)
        live = position >= ctl_ref[2]
        grads, probs, queries, cotangents = [], [], [], []

        def scores_of(head):
            cols = slice(head * HEAD_DIM, (head + 1) * HEAD_DIM)
            query = q_ref[:, cols]
            cotangent = jnp.where(live, d_ref[:, cols], jnp.zeros((), BF16))
            scores = lax.dot_general(key, query, NT, preferred_element_type=F32)
            return cols, query, cotangent, scores

        def finish(cols, query, cotangent, scores):
            row_max = jnp.max(scores, axis=0, keepdims=True)
            powers = jnp.exp2((scores - row_max) * EXP2_SCALE)
            prob = powers * (1.0 / jnp.sum(powers, axis=0, keepdims=True))
            rounded = prob.astype(BF16)
            out_t = lax.dot_general(value_t, rounded, NN, preferred_element_type=F32)
            att_ref[:, cols] = jnp.where(live, out_t.T, 0.0).astype(BF16)
            prob_grad = lax.dot_general(value, cotangent, NT, preferred_element_type=F32)
            delta = jnp.sum(out_t * cotangent.astype(F32).T, axis=0, keepdims=True)
            score_grad = (prob * (prob_grad - delta)).astype(BF16)
            dq_t = lax.dot_general(key_t, score_grad, NN, preferred_element_type=F32)
            dq_ref[:, cols] = (dq_t.T * SCALE).astype(BF16)
            grads.append(score_grad)
            probs.append(rounded)
            queries.append(query)
            cotangents.append(cotangent)

        held = scores_of(0)
        for head in range(heads):
            ahead = scores_of(head + 1) if head + 1 < heads else None
            finish(*held)
            held = ahead
        dk_sum[:length] += jnp.dot(
            jnp.concatenate(grads, axis=1),
            jnp.concatenate(queries, axis=0),
            preferred_element_type=F32,
        )
        dv_sum[:length] += jnp.dot(
            jnp.concatenate(probs, axis=1),
            jnp.concatenate(cotangents, axis=0),
            preferred_element_type=F32,
        )

    for count in range(1, TILES + 1):
        pl.when(ctl_ref[0] == count)(functools.partial(run, count * (img // TILES)))

    @pl.when(step == steps - 1)
    def _():
        dkv_ref[:, :HEAD_DIM] = (dk_sum[...] * SCALE).astype(BF16)
        dkv_ref[:, HEAD_DIM:] = dv_sum[...].astype(BF16)


def attend(ctl, queries, out_grad, keys_values, group, groups, earlier):
    rows, width = queries.shape
    img = keys_values.shape[0]
    heads = 2
    steps = width // groups // HEAD_DIM // heads
    cols = pl.BlockSpec((rows, heads * HEAD_DIM), lambda h, ctl: (0, group * steps + h))
    pair = pl.BlockSpec((img, 2 * HEAD_DIM), lambda h, ctl: (0, 0))
    anywhere = pl.BlockSpec(memory_space=pl.ANY)
    big = jax.ShapeDtypeStruct((rows, width), BF16)
    work = steps * heads * rows * img * HEAD_DIM
    return pl.pallas_call(
        functools.partial(attend_kernel, heads=heads),
        grid_spec=pltpu.PrefetchScalarGridSpec(
            num_scalar_prefetch=1,
            grid=(steps,),
            in_specs=[cols, cols, pair] + [anywhere] * len(earlier),
            out_specs=[cols, cols, pair],
            scratch_shapes=[pltpu.VMEM((HEAD_DIM, img), BF16)] * 2
            + [pltpu.VMEM((img, HEAD_DIM), F32)] * 2,
        ),
        out_shape=[big, big, jax.ShapeDtypeStruct((img, 2 * HEAD_DIM), BF16)],
        input_output_aliases={4 + i: i for i in range(len(earlier))},
        compiler_params=params(1),
        cost_estimate=pl.CostEstimate(
            flops=24 * work, bytes_accessed=8 * rows * width // groups, transcendentals=0
        ),
        name="attend",
    )(ctl, queries, out_grad, keys_values, *earlier)


def norm_back_kernel(parts_ref, pre_ref, gain_ref, out_ref, *, group):
    grad = jnp.sum(parts_ref[...].astype(F32), axis=0)
    head = pre_ref[:, group * HEAD_DIM : (group + 1) * HEAD_DIM]
    factor = lax.rsqrt(jnp.mean(head * head, axis=-1, keepdims=True) + EPSILON)
    gained = gain_ref[...] * grad[:, :HEAD_DIM]
    inner = jnp.mean(head * gained, axis=-1, keepdims=True)
    pre_grad = (factor * gained - factor * factor * factor * head * inner).astype(BF16)
    value_grad = grad[:, HEAD_DIM:].astype(BF16)
    for copy in range(out_ref.shape[0]):
        out_ref[copy, :, :HEAD_DIM] = pre_grad
        out_ref[copy, :, HEAD_DIM:] = value_grad


def norm_back(parts, key_pre, gain, group, copies):
    tokens, width = parts.shape[1:]
    return pl.pallas_call(
        functools.partial(norm_back_kernel, group=group),
        out_shape=jax.ShapeDtypeStruct((copies, tokens, width), BF16),
        compiler_params=pltpu.CompilerParams(vmem_limit_bytes=VMEM_LIMIT),
        name="norm_back",
    )(parts, key_pre, gain)


def turn_kernel(ctl_ref, f_ref, out_ref):
    odd = ctl_ref[3]
    turned = f_ref[...].reshape(-1, f_ref.shape[-1]).T
    rows = out_ref.shape[0]
    spare = turned.shape[0] - rows

    @pl.when(odd == 0)
    def _():
        out_ref[...] = turned[:rows]

    @pl.when(odd != 0)
    def _():
        out_ref[...] = turned[spare:]


def turn(ctl, windows, feat):
    sources, rows, own, width = windows.shape
    tokens = sources * own
    return pl.pallas_call(
        turn_kernel,
        grid_spec=pltpu.PrefetchScalarGridSpec(
            num_scalar_prefetch=1,
            grid=(rows,),
            in_specs=[pl.BlockSpec((sources, 1, own, width), lambda r, ctl: (0, r, 0, 0))],
            out_specs=pl.BlockSpec((feat, tokens), lambda r, ctl: (0, r)),
        ),
        out_shape=jax.ShapeDtypeStruct((feat, rows * tokens), BF16),
        compiler_params=params(1),
        name="turn",
    )(ctl, windows)


def weight_kernel(f_ref, g_ref, out_ref):
    out_ref[...] = jnp.dot(f_ref[...], g_ref[...], preferred_element_type=F32).astype(BF16)


def weight_grad(turned, grads):
    feat, tokens = turned.shape
    width = grads.shape[1]
    return pl.pallas_call(
        weight_kernel,
        out_shape=jax.ShapeDtypeStruct((feat, width), BF16),
        compiler_params=pltpu.CompilerParams(vmem_limit_bytes=VMEM_LIMIT),
        cost_estimate=pl.CostEstimate(
            flops=2 * feat * tokens * width, bytes_accessed=2 * feat * tokens, transcendentals=0
        ),
        name="weight_grad",
    )(turned, grads)


def exchange(array, axes):
    return lax.all_to_all(array, axes, split_axis=0, concat_axis=0, tiled=True)


def on_device(queries, features, w_key, w_value, key_gain, out_grad, tile_counts, text_start):
    dp, seq = lax.axis_size("dp"), lax.axis_size("seq")
    rows, own, feat = features.shape
    text_dev = queries.shape[1]
    kv_dim = w_key.shape[1]
    groups = kv_dim // HEAD_DIM
    tokens = rows * own
    gain = key_gain.reshape(1, HEAD_DIM)
    dp_index, seq_index = lax.axis_index("dp"), lax.axis_index("seq")
    ctl = jnp.stack([tile_counts[0], seq_index * text_dev, text_start[0], dp_index % 2])
    feats = features.reshape(tokens, feat)
    *sends, key_pre, windows = project(feats, w_key, w_value, gain, dp, seq)

    gathered = []
    for send in sends:
        pieces = send.reshape(seq * dp, own, 2 * HEAD_DIM)
        arrived = exchange(pieces, ("seq", "dp"))
        gathered.append(arrived.reshape(seq * tokens, 2 * HEAD_DIM))
    own_pre = exchange(key_pre.reshape(dp, own, kv_dim), "dp").reshape(tokens, kv_dim)
    windows = exchange(windows, "dp").reshape(dp, rows, own, -1)

    earlier = []
    shares = []
    for group in range(groups):
        attended, query_grad, grads = attend(
            ctl, queries[0], out_grad[0], gathered[group], group, groups, earlier
        )
        earlier = [attended, query_grad]
        shares.append(exchange(grads.reshape(seq, tokens, 2 * HEAD_DIM), "seq"))

    turned = turn(ctl, windows, feat // dp)
    key_cols, value_cols = [], []
    for group in range(groups):
        rounded = norm_back(shares[group], own_pre, gain, group, dp)
        everywhere = exchange(rounded, "dp").reshape(dp * tokens, 2 * HEAD_DIM)
        partial = weight_grad(turned, everywhere)
        pieces = exchange(partial.reshape(seq, feat // dp // seq, 2 * HEAD_DIM), "seq")
        summed = jnp.sum(pieces.astype(F32), axis=0)
        key_cols.append(summed[:, :HEAD_DIM])
        value_cols.append(summed[:, HEAD_DIM:])
    return (
        earlier[0][None],
        earlier[1][None],
        jnp.concatenate(key_cols, axis=1),
        jnp.concatenate(value_cols, axis=1),
    )


def solution(mesh):
    placed = (
        P("dp", "seq", "mp"),
        P(None, ("seq", "dp"), None),
        P(None, "mp"),
        P(None, "mp"),
        P(),
        P("dp", "seq", "mp"),
        P("dp"),
        P("dp"),
    )
    return jax.shard_map(
        on_device,
        mesh=mesh,
        in_specs=placed,
        out_specs=(
            P("dp", "seq", "mp"),
            P("dp", "seq", "mp"),
            P(("dp", "seq"), "mp"),
            P(("dp", "seq"), "mp"),
        ),
        check_vma=False,
    )
```

time: 737 us -> 190 us (0.26)
  waiting for transfers between devices: 463 us -> 60.8 us
  local copies, waits for them, and re-layouts: 76.4 us -> 9.64 us
  matrix products: 64.6 us -> 0 us
  other arithmetic: 37.7 us -> 0.92 us
  Pallas kernels: 0 us -> 35.9 us
  starting transfers between devices: 7.91 us -> 37.3 us
  between operations: 15.6 us -> 2.08 us
  blocking collectives: 54.8 us -> 42.4 us
  loops' own time: 11.8 us -> 0 us
    unnamed x10 -> x0, waiting for transfers between devices: 455 us -> none
    dot_general x27 -> x0, matrix products: 64.6 us -> none  [the longest x4 11.2 us: group_pass(): jnp.dot(grad_live, v_group.T, preferred_element_type=jnp.float32)]
    all_gather x2 -> x0, blocking collectives: 54.8 us -> none  [the longest x1 29 us: on_device(): lax.all_gather(values_here, 'seq', axis=0, tiled=True)]
    all_to_all x1 -> x8, waiting for transfers between devices: 8.26 us -> 60.8 us  [exchange(): return lax.all_to_all(array, axes, split_axis=0, concat_axis=0, tiled=True)]
    all_to_all x0 -> x2, blocking collectives: none -> 42.4 us  [exchange(): return lax.all_to_all(array, axes, split_axis=0, concat_axis=0, tiled=True)]
    pallas_call x0 -> x8, Pallas kernels: none -> 35.9 us  [the longest x2 22.8 us: attend(): pl.pallas_call(functools.partial(attend_kernel, heads=heads), grid_spec=p...]
    all_to_all x1 -> x8, starting transfers between devices: 7.71 us -> 37.3 us  [exchange(): return lax.all_to_all(array, axes, split_axis=0, concat_axis=0, tiled=True)]
    another operation x9 -> x0, local copies, waits for them, and re-layouts: 22.2 us -> none  [the longest x2 7.45 us: on_device(): jnp.stack(query_parts, axis=2).reshape(1, text_dev, kv_dim * group_size)]
  transfers between devices with their start and end apart: 6 -> 8, of which waited for: 5 -> 6; matrix products, arithmetic and copies ran while one was open for 14% -> 0% of each run, Pallas kernels for 0% -> 16%
where the time goes in v1:
time: 190 us; the launch traced here: 189 us
  waiting for transfers between devices  60.8 us (32%)
  blocking collectives  42.4 us (22%)
  starting transfers between devices  37.3 us (20%)
  Pallas kernels  35.9 us (19%)
  local copies, waits for them, and re-layouts  9.64 us (5%)
  between operations  2.08 us (1%)
    all_to_all x8, waiting for transfers between devices, exchange(): return lax.all_to_all(array, axes, split_axis=0, concat_axis=0, tiled=True)  60.8 us
    all_to_all x2, blocking collectives, exchange(): return lax.all_to_all(array, axes, split_axis=0, concat_axis=0, tiled=True)  42.4 us
    all_to_all x8, starting transfers between devices, exchange(): return lax.all_to_all(array, axes, split_axis=0, concat_axis=0, tiled=True)  37.3 us
    pallas_call x2, Pallas kernels, attend(): pl.pallas_call(functools.partial(attend_kernel, heads=heads), grid_spec=p...  22.8 us
    unnamed x18, local copies, waits for them, and re-layouts  9.62 us
    pallas_call x1, Pallas kernels, project(): pl.pallas_call(functools.partial(project_kernel, windows=windows, per_ste...  6.61 us
  transfers between devices with their start and end apart: 8, of which 6 were waited for; matrix products, arithmetic and copies ran while one was open for 0% of the time, Pallas kernels for 16%

profile of v1, /device:TPU:0, one launch (start us, length us, event | category | flops | bytes accessed | tf_op | source)
XLA Modules:
  0.0 189.0 jit_solution(555649286263705186)
XLA Ops:
  0.6 0.0 copy-start.3
  0.6 1.5 copy-done.3
  2.2 0.0 copy-start.4
  2.2 0.7 copy-done.4
  2.8 6.6 %project.1 = (bf16[8,128,256]{2,1,0:T(8,128)(2,1)}, bf16[8,128,256]{2,1,0:T(8,128)(2,1)}, f32[128,256]{1,0:T(8,128)S(1)}, bf16[8,128,1024]{2,1,0:T(8,128)(2,1)S(1)}) custom-call(bf16[128,7680]{1,0:T(8,128)(2,1)S(1)} %bitcast.24, bf16[7680,256]{1,0:T(8,128)(2,1)} %wk_ref.1, bf16[7680,256]{1,0:T(8,128)(2,1)} %wv_ref.1, f32[1,128]{1,0:T(1,128)S(1)} %bitcast.30), custom_call_target="tpu_custom_call" | custom-call | flops 1006632960 | bytes 11796480 | tf_op jit(solution)/shard_map/project/pallas_call | solution.py:82
  9.4 0.0 copy-start.2
  9.4 1.3 copy-done.2
  10.8 0.0 copy-start.6
  10.8 15.7 %all_to_all.50 = f32[8,16,256]{2,1,0:T(8,128)S(1)} all-to-all(f32[8,16,256]{2,1,0:T(8,128)S(1)} %bitcast.29), channel_id=1, replica_groups=mesh['dp'=8,'seq'=8,'mp'=2] {'dp'}, dimensions={0} | all-to-all | bytes 262144 | tf_op jit(solution)/shard_map/all_to_all | solution.py:287
  26.5 6.7 %all-to-all-start.1 = ((bf16[64,16,256]{2,1,0:T(8,128)(2,1)}), bf16[64,16,256]{2,1,0:T(8,128)(2,1)S(1)}, u32[]{:S(2)}, u32[]{:S(2)}) async-start(bf16[64,16,256]{2,1,0:T(8,128)(2,1)} %bitcast.8), calls=%async_computation.1 | async-start | bytes 1048576 | tf_op jit(solution)/shard_map/all_to_all | solution.py:287
  34.4 0.1 pad_add_fusion.ctl_ref
  34.5 10.3 %all-to-all-done.1 = bf16[64,16,256]{2,1,0:T(8,128)(2,1)S(1)} async-done(((bf16[64,16,256]{2,1,0:T(8,128)(2,1)}), bf16[64,16,256]{2,1,0:T(8,128)(2,1)S(1)}, u32[]{:S(2)}, u32[]{:S(2)}) %all-to-all-start.1) | async-done | bytes 524320 | tf_op jit(solution)/shard_map/all_to_all | solution.py:287
  44.9 5.5 %all-to-all-start = ((bf16[64,16,256]{2,1,0:T(8,128)(2,1)}), bf16[64,16,256]{2,1,0:T(8,128)(2,1)S(1)}, u32[]{:S(2)}, u32[]{:S(2)}) async-start(bf16[64,16,256]{2,1,0:T(8,128)(2,1)} %bitcast.6), calls=%async_computation | async-start | bytes 1048576 | tf_op jit(solution)/shard_map/all_to_all | solution.py:287
  50.4 0.0 copy-done.6
  50.4 0.0 copy-start.7
  50.4 1.6 copy-done.7
  52.0 11.4 %attend.2 = (bf16[512,2048]{1,0:T(8,128)(2,1)}, bf16[512,2048]{1,0:T(8,128)(2,1)}, bf16[1024,256]{1,0:T(8,128)(2,1)}) custom-call(s32[4]{0:T(128)S(1)} %pad_add_fusion.ctl_ref, bf16[512,2048]{1,0:T(8,128)(2,1)S(1)} %bitcast.33, bf16[512,2048]{1,0:T(8,128)(2,1)S(1)} %bitcast.35, bf16[1024,256]{1,0:T(8,128)(2,1)S(1)} %bitcast.27), custom_call_target="tpu_custom_call" | custom-call | flops 12884901888 | bytes 4194304 | tf_op jit(solution)/shard_map/attend/pallas_call | solution.py:193
  63.4 0.0 all-to-all-done
  63.4 5.3 %all-to-all-start.3 = ((bf16[8,128,256]{2,1,0:T(8,128)(2,1)}), bf16[8,128,256]{2,1,0:T(8,128)(2,1)S(1)}, u32[]{:S(2)}, u32[]{:S(2)}) async-start(bf16[8,128,256]{2,1,0:T(8,128)(2,1)} %bitcast.13), calls=%async_computation.3 | async-start | bytes 1048576 | tf_op jit(solution)/shard_map/all_to_all | solution.py:287
  68.7 0.0 copy-start.8
  68.7 1.6 copy-done.8
  70.3 0.0 copy-start.5
  70.3 11.4 %attend.3 = (bf16[512,2048]{1,0:T(8,128)(2,1)}, bf16[512,2048]{1,0:T(8,128)(2,1)}, bf16[1024,256]{1,0:T(8,128)(2,1)}) custom-call(s32[4]{0:T(128)S(1)} %pad_add_fusion.ctl_ref, bf16[512,2048]{1,0:T(8,128)(2,1)S(1)} %bitcast.34, bf16[512,2048]{1,0:T(8,128)(2,1)S(1)} %bitcast.36, ...), custom_call_target="tpu_custom_call", output_to_operand_aliasing={{0}: (4, {}), {1}: (5, {})} | custom-call | flops 12884901888 | bytes 4194304 | tf_op jit(solution)/shard_map/attend/pallas_call | solution.py:193
  81.7 0.0 all-to-all-done.3.parts_ref
  81.7 5.7 %all-to-all-start.7 = ((bf16[8,128,256]{2,1,0:T(8,128)(2,1)}), bf16[8,128,256]{2,1,0:T(8,128)(2,1)S(1)}, u32[]{:S(2)}, u32[]{:S(2)}) async-start(bf16[8,128,256]{2,1,0:T(8,128)(2,1)} %bitcast.18), calls=%async_computation.7 | async-start | bytes 1048576 | tf_op jit(solution)/shard_map/all_to_all | solution.py:287
  87.4 0.0 copy-done.5
  87.4 0.2 norm_back.2
  87.5 8.5 %all-to-all-done.7.parts_ref = bf16[8,128,256]{2,1,0:T(8,128)(2,1)S(1)} async-done(((bf16[8,128,256]{2,1,0:T(8,128)(2,1)}), bf16[8,128,256]{2,1,0:T(8,128)(2,1)S(1)}, u32[]{:S(2)}, u32[]{:S(2)}) %all-to-all-start.7) | async-done | bytes 524320 | tf_op jit(solution)/shard_map/all_to_all | solution.py:287
  96.1 26.7 %all_to_all.51 = bf16[8,128,256]{2,1,0:T(8,128)(2,1)S(1)} all-to-all(bf16[8,128,256]{2,1,0:T(8,128)(2,1)S(1)} %norm_back.2), channel_id=1, replica_groups=mesh['dp'=8,'seq'=8,'mp'=2] {'dp'}, dimensions={0} | all-to-all | bytes 1048576 | tf_op jit(solution)/shard_map/all_to_all | solution.py:287
  122.8 3.6 %all-to-all-start.2 = ((bf16[8,128,1024]{2,1,0:T(8,128)(2,1)}), bf16[8,128,1024]{2,1,0:T(8,128)(2,1)S(1)}, u32[]{:S(2)}, u32[]{:S(2)}) async-start(bf16[8,128,1024]{2,1,0:T(8,128)(2,1)} %copy-done.2), calls=%async_computation.2 | async-start | bytes 4194304 | tf_op jit(solution)/shard_map/all_to_all | solution.py:287
  126.4 1.0 norm_back.3
  127.3 22.1 %all-to-all-done.2 = bf16[8,128,1024]{2,1,0:T(8,128)(2,1)S(1)} async-done(((bf16[8,128,1024]{2,1,0:T(8,128)(2,1)}), bf16[8,128,1024]{2,1,0:T(8,128)(2,1)S(1)}, u32[]{:S(2)}, u32[]{:S(2)}) %all-to-all-start.2) | async-done | bytes 2097184 | tf_op jit(solution)/shard_map/all_to_all | solution.py:287
  149.4 0.0 copy-start
  149.4 1.3 copy-done
  150.7 3.5 %all-to-all-start.8 = ((bf16[8,128,256]{2,1,0:T(8,128)(2,1)}), bf16[8,128,256]{2,1,0:T(8,128)(2,1)S(1)}, u32[]{:S(2)}, u32[]{:S(2)}) async-start(bf16[8,128,256]{2,1,0:T(8,128)(2,1)} %norm_back.3), calls=%async_computation.8 | async-start | bytes 1048576 | tf_op jit(solution)/shard_map/all_to_all | solution.py:287
  154.2 0.0 copy-start.1
  154.2 1.6 copy-done.1
  155.8 2.5 %turn.1.f_ref = bf16[960,1024]{1,0:T(8,128)(2,1)S(1)} custom-call(s32[4]{0:T(128)S(1)} %pad_add_fusion.ctl_ref, bf16[8,8,16,1024]{3,2,1,0:T(8,128)(2,1)S(1)} %bitcast.21), custom_call_target="tpu_custom_call" | custom-call | tf_op jit(solution)/shard_map/turn/pallas_call | solution.py:254
  158.3 1.5 weight_grad.2
  159.8 4.6 %all-to-all-done.8 = bf16[8,128,256]{2,1,0:T(8,128)(2,1)S(1)} async-done(((bf16[8,128,256]{2,1,0:T(8,128)(2,1)}), bf16[8,128,256]{2,1,0:T(8,128)(2,1)S(1)}, u32[]{:S(2)}, u32[]{:S(2)}) %all-to-all-start.8) | async-done | bytes 524320 | tf_op jit(solution)/shard_map/all_to_all | solution.py:287
  164.4 3.5 %all-to-all-start.6 = ((bf16[8,120,256]{2,1,0:T(8,128)(2,1)}), bf16[8,120,256]{2,1,0:T(8,128)(2,1)S(1)}, u32[]{:S(2)}, u32[]{:S(2)}) async-start(bf16[8,120,256]{2,1,0:T(8,128)(2,1)} %bitcast.17), calls=%async_computation.6 | async-start | bytes 983040 | tf_op jit(solution)/shard_map/all_to_all | solution.py:287
  167.8 1.5 weight_grad.3
  169.3 7.0 %all-to-all-done.6 = bf16[8,120,256]{2,1,0:T(8,128)(2,1)S(1)} async-done(((bf16[8,120,256]{2,1,0:T(8,128)(2,1)}), bf16[8,120,256]{2,1,0:T(8,128)(2,1)S(1)}, u32[]{:S(2)}, u32[]{:S(2)}) %all-to-all-start.6) | async-done | bytes 491552 | tf_op jit(solution)/shard_map/all_to_all | solution.py:287
  176.3 3.5 %all-to-all-start.9 = ((bf16[8,120,256]{2,1,0:T(8,128)(2,1)}), bf16[8,120,256]{2,1,0:T(8,128)(2,1)S(1)}, u32[]{:S(2)}, u32[]{:S(2)}) async-start(bf16[8,120,256]{2,1,0:T(8,128)(2,1)} %bitcast.20), calls=%async_computation.9 | async-start | bytes 983040 | tf_op jit(solution)/shard_map/all_to_all | solution.py:287
  179.8 0.1 convert_reduce_fusion.1
  179.9 8.4 %all-to-all-done.9 = bf16[8,120,256]{2,1,0:T(8,128)(2,1)S(1)} async-done(((bf16[8,120,256]{2,1,0:T(8,128)(2,1)}), bf16[8,120,256]{2,1,0:T(8,128)(2,1)S(1)}, u32[]{:S(2)}, u32[]{:S(2)}) %all-to-all-start.9) | async-done | bytes 491552 | tf_op jit(solution)/shard_map/all_to_all | solution.py:287
  188.2 0.1 convert_reduce_fusion
  188.3 0.7 pad_maximum_fusion
  (2 shorter events, 0.0 us)
Async XLA Ops:
  0.6 1.5 copy-start.3
  2.2 0.7 copy-start.4
  9.4 1.3 copy-start.2
  10.8 39.6 %copy-start.6 = (bf16[1,512,2048]{2,1,0:T(8,128)(2,1)S(1)}, bf16[1,512,2048]{2,1,0:T(8,128)(2,1)}, u32[]{:S(2)}) copy-start(bf16[1,512,2048]{2,1,0:T(8,128)(2,1)} %param.8) | copy-start | bytes 6291460
  26.5 18.4 %all-to-all-start.1 = ((bf16[64,16,256]{2,1,0:T(8,128)(2,1)}), bf16[64,16,256]{2,1,0:T(8,128)(2,1)S(1)}, u32[]{:S(2)}, u32[]{:S(2)}) async-start(bf16[64,16,256]{2,1,0:T(8,128)(2,1)} %bitcast.8), calls=%async_computation.1 | async-start | bytes 1048576 | tf_op jit(solution)/shard_map/all_to_all | solution.py:287
  44.9 18.5 %all-to-all-start = ((bf16[64,16,256]{2,1,0:T(8,128)(2,1)}), bf16[64,16,256]{2,1,0:T(8,128)(2,1)S(1)}, u32[]{:S(2)}, u32[]{:S(2)}) async-start(bf16[64,16,256]{2,1,0:T(8,128)(2,1)} %bitcast.6), calls=%async_computation | async-start | bytes 1048576 | tf_op jit(solution)/shard_map/all_to_all | solution.py:287
  50.4 1.6 copy-start.7
  63.4 18.3 %all-to-all-start.3 = ((bf16[8,128,256]{2,1,0:T(8,128)(2,1)}), bf16[8,128,256]{2,1,0:T(8,128)(2,1)S(1)}, u32[]{:S(2)}, u32[]{:S(2)}) async-start(bf16[8,128,256]{2,1,0:T(8,128)(2,1)} %bitcast.13), calls=%async_computation.3 | async-start | bytes 1048576 | tf_op jit(solution)/shard_map/all_to_all | solution.py:287
  68.7 1.6 copy-start.8
  70.3 17.1 %copy-start.5 = (f32[128]{0:T(128)S(1)}, f32[128]{0:T(128)}, u32[]{:S(2)}) copy-start(f32[128]{0:T(128)} %param.12) | copy-start | bytes 1540
  81.7 14.4 %all-to-all-start.7 = ((bf16[8,128,256]{2,1,0:T(8,128)(2,1)}), bf16[8,128,256]{2,1,0:T(8,128)(2,1)S(1)}, u32[]{:S(2)}, u32[]{:S(2)}) async-start(bf16[8,128,256]{2,1,0:T(8,128)(2,1)} %bitcast.18), calls=%async_computation.7 | async-start | bytes 1048576 | tf_op jit(solution)/shard_map/all_to_all | solution.py:287
  122.8 26.6 %all-to-all-start.2 = ((bf16[8,128,1024]{2,1,0:T(8,128)(2,1)}), bf16[8,128,1024]{2,1,0:T(8,128)(2,1)S(1)}, u32[]{:S(2)}, u32[]{:S(2)}) async-start(bf16[8,128,1024]{2,1,0:T(8,128)(2,1)} %copy-done.2), calls=%async_computation.2 | async-start | bytes 4194304 | tf_op jit(solution)/shard_map/all_to_all | solution.py:287
  149.4 1.3 copy-start
  150.7 13.6 %all-to-all-start.8 = ((bf16[8,128,256]{2,1,0:T(8,128)(2,1)}), bf16[8,128,256]{2,1,0:T(8,128)(2,1)S(1)}, u32[]{:S(2)}, u32[]{:S(2)}) async-start(bf16[8,128,256]{2,1,0:T(8,128)(2,1)} %norm_back.3), calls=%async_computation.8 | async-start | bytes 1048576 | tf_op jit(solution)/shard_map/all_to_all | solution.py:287
  154.2 1.6 copy-start.1
  164.4 11.9 %all-to-all-start.6 = ((bf16[8,120,256]{2,1,0:T(8,128)(2,1)}), bf16[8,120,256]{2,1,0:T(8,128)(2,1)S(1)}, u32[]{:S(2)}, u32[]{:S(2)}) async-start(bf16[8,120,256]{2,1,0:T(8,128)(2,1)} %bitcast.17), calls=%async_computation.6 | async-start | bytes 983040 | tf_op jit(solution)/shard_map/all_to_all | solution.py:287
  176.3 11.9 %all-to-all-start.9 = ((bf16[8,120,256]{2,1,0:T(8,128)(2,1)}), bf16[8,120,256]{2,1,0:T(8,128)(2,1)S(1)}, u32[]{:S(2)}, u32[]{:S(2)}) async-start(bf16[8,120,256]{2,1,0:T(8,128)(2,1)} %bitcast.20), calls=%async_computation.9 | async-start | bytes 983040 | tf_op jit(solution)/shard_map/all_to_all | solution.py:287

commit v2 on v1

v2 whole, which is shorter than its diff:
```python
import functools

import jax
import jax.numpy as jnp
from jax import lax
from jax.experimental import pallas as pl
from jax.experimental.pallas import tpu as pltpu
from jax.sharding import PartitionSpec as P

HEAD_DIM = 128
TILES = 4
EPSILON = 1e-05
SCALE = HEAD_DIM**-0.5
EXP2_SCALE = SCALE * 1.4426950408889634
BF16 = jnp.bfloat16
F32 = jnp.float32
LANES = 128
VMEM_LIMIT = 60 * 2**20

NN = (((1,), (0,)), ((), ()))
NT = (((1,), (1,)), ((), ()))


def whole(shape):
    return pl.BlockSpec(shape, lambda *_: (0,) * len(shape))


def params(axes):
    return pltpu.CompilerParams(
        vmem_limit_bytes=VMEM_LIMIT, dimension_semantics=("arbitrary",) * axes
    )


def project_kernel(f_ref, wk_ref, wv_ref, gain_ref, send_ref, win_ref, total):
    step, steps = pl.program_id(0), pl.num_programs(0)
    depth, kv_dim = wk_ref.shape
    windows, tokens, width = win_ref.shape
    tiles = f_ref.shape[1] // LANES
    own = tokens // windows
    part = f_ref[:, pl.ds(pl.multiple_of(step * depth, LANES), depth)]

    @pl.when(step == 0)
    def _():
        total[...] = jnp.zeros_like(total)

    total[:, :kv_dim] += jnp.dot(part, wk_ref[...], preferred_element_type=F32)
    total[:, kv_dim:] += jnp.dot(part, wv_ref[...], preferred_element_type=F32)

    @pl.when(step < windows // 2)
    def _():
        for inner in range(2):
            at = step * 2 + inner
            tile = (at * tiles) // windows
            win_ref[at] = f_ref[:, pl.ds(pl.multiple_of(tile * LANES, LANES), width)]

    @pl.when(step == steps - 1)
    def _():
        for group in range(kv_dim // HEAD_DIM):
            cols = slice(group * HEAD_DIM, (group + 1) * HEAD_DIM)
            head = total[:, cols]
            factor = lax.rsqrt(jnp.mean(head * head, axis=-1, keepdims=True) + EPSILON)
            key = (head * factor * gain_ref[...]).astype(BF16)
            start = kv_dim + group * HEAD_DIM
            value = total[:, start : start + HEAD_DIM].astype(BF16)
            at = 2 * group * HEAD_DIM
            for copy in range(send_ref.shape[0]):
                send_ref[copy, :, at : at + HEAD_DIM] = key
                send_ref[copy, :, at + HEAD_DIM : at + 2 * HEAD_DIM] = value
        lane = lax.broadcasted_iota(jnp.int32, (own, LANES), 1)
        half = LANES // 2
        for window in range(windows):
            head = total[window * own : (window + 1) * own, :kv_dim]
            high = head.astype(BF16).astype(F32)
            pair = jnp.concatenate([high, head - high], axis=1)
            place = 1 - window % 2
            at = (width - LANES) * place
            for block in range(windows):
                piece = pair[:, block // 2 * LANES : (block // 2 + 1) * LANES]
                if block % 2 != place:
                    piece = pltpu.roll(piece, half, axis=1)
                rows = slice(block * own, (block + 1) * own)
                kept = win_ref[window, rows, at : at + LANES].astype(F32)
                mixed = jnp.where((lane >= half) == bool(place), piece, kept)
                win_ref[window, rows, at : at + LANES] = mixed.astype(BF16)


def project(feats, w_key, w_value, gain, windows, copies):
    tokens, feat = feats.shape
    kv_dim = w_key.shape[1]
    steps = windows // 2 + 1
    depth = feat // steps
    width = -(-(feat // windows) // LANES) * LANES
    outs = [(copies, tokens, 2 * kv_dim), (windows, tokens, width)]
    return pl.pallas_call(
        project_kernel,
        grid=(steps,),
        in_specs=[
            whole((tokens, feat)),
            pl.BlockSpec((depth, kv_dim), lambda k: (k, 0)),
            pl.BlockSpec((depth, kv_dim), lambda k: (k, 0)),
            whole((1, HEAD_DIM)),
        ],
        out_specs=[whole(shape) for shape in outs],
        out_shape=[jax.ShapeDtypeStruct(shape, BF16) for shape in outs],
        scratch_shapes=[pltpu.VMEM((tokens, 2 * kv_dim), F32)],
        compiler_params=params(1),
        cost_estimate=pl.CostEstimate(
            flops=4 * tokens * feat * kv_dim,
            bytes_accessed=4 * feat * kv_dim + 4 * tokens * feat,
            transcendentals=0,
        ),
        name="project",
    )(feats, w_key, w_value, gain)


def attend_kernel(
    ctl_ref, q_ref, d_ref, kv_ref, att_ref, dq_ref, dkv_ref, kt_ref, vt_ref, dk_sum, dv_sum, *, heads
):
    step, steps = pl.program_id(1), pl.num_programs(1)
    rows = q_ref.shape[0]
    img = kv_ref.shape[0]

    @pl.when(step == 0)
    def _():
        dk_sum[...] = jnp.zeros_like(dk_sum)
        dv_sum[...] = jnp.zeros_like(dv_sum)
        kt_ref[...] = kv_ref[:, :HEAD_DIM].T
        vt_ref[...] = kv_ref[:, HEAD_DIM:].T

    def run(length):
        key, value = kv_ref[:length, :HEAD_DIM], kv_ref[:length, HEAD_DIM:]
        key_t, value_t = kt_ref[:, :length], vt_ref[:, :length]
        position = ctl_ref[1] + lax.broadcasted_iota(jnp.int32, (rows, HEAD_DIM), 0)
        live = position >= ctl_ref[2]
        grads, probs, queries, cotangents = [], [], [], []

        def scores_of(head):
            cols = slice(head * HEAD_DIM, (head + 1) * HEAD_DIM)
            query = q_ref[:, cols]
            cotangent = jnp.where(live, d_ref[:, cols], jnp.zeros((), BF16))
            scores = lax.dot_general(key, query, NT, preferred_element_type=F32)
            return cols, query, cotangent, scores

        def finish(cols, query, cotangent, scores):
            row_max = jnp.max(scores, axis=0, keepdims=True)
            powers = jnp.exp2((scores - row_max) * EXP2_SCALE)
            prob = powers * (1.0 / jnp.sum(powers, axis=0, keepdims=True))
            rounded = prob.astype(BF16)
            out_t = lax.dot_general(value_t, rounded, NN, preferred_element_type=F32)
            att_ref[:, cols] = jnp.where(live, out_t.T, 0.0).astype(BF16)
            prob_grad = lax.dot_general(value, cotangent, NT, preferred_element_type=F32)
            delta = jnp.sum(prob * prob_grad, axis=0, keepdims=True)
            score_grad = (prob * (prob_grad - delta)).astype(BF16)
            dq_t = lax.dot_general(key_t, score_grad, NN, preferred_element_type=F32)
            dq_ref[:, cols] = (dq_t.T * SCALE).astype(BF16)
            grads.append(score_grad)
            probs.append(rounded)
            queries.append(query)
            cotangents.append(cotangent)

        held = scores_of(0)
        for head in range(heads):
            ahead = scores_of(head + 1) if head + 1 < heads else None
            finish(*held)
            held = ahead
        dk_sum[:length] += jnp.dot(
            jnp.concatenate(grads, axis=1),
            jnp.concatenate(queries, axis=0),
            preferred_element_type=F32,
        )
        dv_sum[:length] += jnp.dot(
            jnp.concatenate(probs, axis=1),
            jnp.concatenate(cotangents, axis=0),
            preferred_element_type=F32,
        )

    for count in range(1, TILES + 1):
        pl.when(ctl_ref[0] == count)(functools.partial(run, count * (img // TILES)))

    @pl.when(step == steps - 1)
    def _():
        dkv_ref[:, :HEAD_DIM] = (dk_sum[...] * SCALE).astype(BF16)
        dkv_ref[:, HEAD_DIM:] = dv_sum[...].astype(BF16)


def attend(ctl, queries, out_grad, keys_values):
    rows, width = queries.shape
    img, pairs = keys_values.shape
    groups = pairs // (2 * HEAD_DIM)
    heads = 2
    steps = width // groups // HEAD_DIM // heads
    cols = pl.BlockSpec((rows, heads * HEAD_DIM), lambda g, h, ctl: (0, g * steps + h))
    pair = pl.BlockSpec((img, 2 * HEAD_DIM), lambda g, h, ctl: (0, g))
    big = jax.ShapeDtypeStruct((rows, width), BF16)
    return pl.pallas_call(
        functools.partial(attend_kernel, heads=heads),
        grid_spec=pltpu.PrefetchScalarGridSpec(
            num_scalar_prefetch=1,
            grid=(groups, steps),
            in_specs=[cols, cols, pair],
            out_specs=[cols, cols, pair],
            scratch_shapes=[pltpu.VMEM((HEAD_DIM, img), BF16)] * 2
            + [pltpu.VMEM((img, HEAD_DIM), F32)] * 2,
        ),
        out_shape=[big, big, jax.ShapeDtypeStruct((img, pairs), BF16)],
        compiler_params=params(2),
        cost_estimate=pl.CostEstimate(
            flops=24 * rows * width * img, bytes_accessed=8 * rows * width, transcendentals=0
        ),
        name="attend",
    )(ctl, queries, out_grad, keys_values)


def norm_back_kernel(ctl_ref, parts_ref, pre_ref, gain_ref, out_ref):
    grad = jnp.sum(parts_ref[...].astype(F32), axis=0)
    tokens, width = grad.shape
    place = 1 - ctl_ref[3]
    half = LANES // 2
    lane = lax.broadcasted_iota(jnp.int32, (tokens, LANES), 1)
    blocks = pre_ref.shape[1] // 2

    def piece(block):
        high = pre_ref[:, block].astype(F32).reshape(tokens, LANES)
        low = pre_ref[:, blocks + block].astype(F32).reshape(tokens, LANES)
        held = high + low
        return jnp.where(place == block % 2, held, pltpu.roll(held, half, axis=1))

    for group in range(width // (2 * HEAD_DIM)):
        head = jnp.where(lane < half, piece(2 * group), piece(2 * group + 1))
        at = 2 * group * HEAD_DIM
        key_grad = grad[:, at : at + HEAD_DIM]
        factor = lax.rsqrt(jnp.mean(head * head, axis=-1, keepdims=True) + EPSILON)
        gained = gain_ref[...] * key_grad
        inner = jnp.mean(head * gained, axis=-1, keepdims=True)
        pre_grad = (factor * gained - factor * factor * factor * head * inner).astype(BF16)
        value_grad = grad[:, at + HEAD_DIM : at + 2 * HEAD_DIM].astype(BF16)
        for copy in range(out_ref.shape[0]):
            out_ref[copy, :, at : at + HEAD_DIM] = pre_grad
            out_ref[copy, :, at + HEAD_DIM : at + 2 * HEAD_DIM] = value_grad


def norm_back(ctl, parts, windows, gain, copies):
    tokens, width = parts.shape[1:]
    sources, rows, own, lanes = windows.shape
    last = lanes // LANES - 1
    return pl.pallas_call(
        norm_back_kernel,
        grid_spec=pltpu.PrefetchScalarGridSpec(
            num_scalar_prefetch=1,
            grid=(1,),
            in_specs=[
                whole(parts.shape),
                pl.BlockSpec(
                    (sources, rows, own, LANES), lambda i, ctl: (0, 0, 0, last * (1 - ctl[3]))
                ),
                whole(gain.shape),
            ],
            out_specs=whole((copies, tokens, width)),
        ),
        out_shape=jax.ShapeDtypeStruct((copies, tokens, width), BF16),
        name="norm_back",
    )(ctl, parts, windows, gain)


def turn_kernel(ctl_ref, f_ref, out_ref):
    odd = ctl_ref[3]
    turned = f_ref[...].reshape(-1, f_ref.shape[-1]).T
    rows = out_ref.shape[0]
    spare = turned.shape[0] - rows

    @pl.when(odd == 0)
    def _():
        out_ref[...] = turned[:rows]

    @pl.when(odd != 0)
    def _():
        out_ref[...] = turned[spare:]


def turn(ctl, windows, feat):
    sources, rows, own, width = windows.shape
    tokens = sources * own
    return pl.pallas_call(
        turn_kernel,
        grid_spec=pltpu.PrefetchScalarGridSpec(
            num_scalar_prefetch=1,
            grid=(rows,),
            in_specs=[pl.BlockSpec((sources, 1, own, width), lambda r, ctl: (0, r, 0, 0))],
            out_specs=pl.BlockSpec((feat, tokens), lambda r, ctl: (0, r)),
        ),
        out_shape=jax.ShapeDtypeStruct((feat, rows * tokens), BF16),
        compiler_params=params(1),
        name="turn",
    )(ctl, windows)


def weight_kernel(f_ref, g_ref, out_ref):
    out_ref[...] = jnp.dot(f_ref[...], g_ref[...], preferred_element_type=F32).astype(BF16)


def weight_grad(turned, grads):
    feat, tokens = turned.shape
    width = grads.shape[1]
    return pl.pallas_call(
        weight_kernel,
        out_shape=jax.ShapeDtypeStruct((feat, width), BF16),
        compiler_params=pltpu.CompilerParams(vmem_limit_bytes=VMEM_LIMIT),
        cost_estimate=pl.CostEstimate(
            flops=2 * feat * tokens * width, bytes_accessed=2 * feat * tokens, transcendentals=0
        ),
        name="weight_grad",
    )(turned, grads)


def finish_kernel(parts_ref, key_ref, value_ref):
    total = jnp.sum(parts_ref[...].astype(F32), axis=0)
    for group in range(total.shape[1] // (2 * HEAD_DIM)):
        cols = slice(group * HEAD_DIM, (group + 1) * HEAD_DIM)
        at = 2 * group * HEAD_DIM
        key_ref[:, cols] = total[:, at : at + HEAD_DIM]
        value_ref[:, cols] = total[:, at + HEAD_DIM : at + 2 * HEAD_DIM]


def finish(parts):
    out = jax.ShapeDtypeStruct((parts.shape[1], parts.shape[2] // 2), F32)
    return pl.pallas_call(finish_kernel, out_shape=[out, out], name="finish")(parts)


def exchange(array, axes):
    return lax.all_to_all(array, axes, split_axis=0, concat_axis=0, tiled=True)


def on_device(queries, features, w_key, w_value, key_gain, out_grad, tile_counts, text_start):
    dp, seq = lax.axis_size("dp"), lax.axis_size("seq")
    rows, own, feat = features.shape
    text_dev = queries.shape[1]
    pairs = 2 * w_key.shape[1]
    tokens = rows * own
    gain = key_gain.reshape(1, HEAD_DIM)
    dp_index, seq_index = lax.axis_index("dp"), lax.axis_index("seq")
    ctl = jnp.stack([tile_counts[0], seq_index * text_dev, text_start[0], dp_index & 1])
    feats = features.reshape(tokens, feat)
    send, windows = project(feats, w_key, w_value, gain, dp, seq)
    arrived = exchange(send.reshape(seq * dp, own, pairs), ("seq", "dp"))
    windows, arrived = lax.optimization_barrier((windows, arrived))
    keys_values = arrived.reshape(seq * tokens, pairs)
    windows = exchange(windows, "dp").reshape(dp, rows, own, -1)
    attended, query_grad, grads = attend(ctl, queries[0], out_grad[0], keys_values)
    shares = exchange(grads.reshape(seq, tokens, pairs), "seq")
    turned = turn(ctl, windows, feat // dp)
    rounded = norm_back(ctl, shares, windows, gain, dp)
    everywhere = exchange(rounded, "dp").reshape(dp * tokens, pairs)
    partial = weight_grad(turned, everywhere)
    pieces = exchange(partial.reshape(seq, feat // dp // seq, pairs), "seq")
    key_weight, value_weight = finish(pieces)
    return attended[None], query_grad[None], key_weight, value_weight


def solution(mesh):
    placed = (
        P("dp", "seq", "mp"),
        P(None, ("seq", "dp"), None),
        P(None, "mp"),
        P(None, "mp"),
        P(),
        P("dp", "seq", "mp"),
        P("dp"),
        P("dp"),
    )
    return jax.shard_map(
        on_device,
        mesh=mesh,
        in_specs=placed,
        out_specs=(
            P("dp", "seq", "mp"),
            P("dp", "seq", "mp"),
            P(("dp", "seq"), "mp"),
            P(("dp", "seq"), "mp"),
        ),
        check_vma=False,
    )
```

time: 190 us -> 171 us (0.900)
  waiting for transfers between devices: 60.8 us -> 22.8 us
  blocking collectives: 42.4 us -> 80 us
  starting transfers between devices: 37.3 us -> 15 us
  Pallas kernels: 35.9 us -> 47.8 us
  local copies, waits for them, and re-layouts: 9.64 us -> 1.94 us
    all_to_all x8 -> x2, waiting for transfers between devices: 60.8 us -> 22.8 us  [exchange(): return lax.all_to_all(array, axes, split_axis=0, concat_axis=0, tiled=True)]
    all_to_all x2 -> x3, blocking collectives: 42.4 us -> 80 us  [exchange(): return lax.all_to_all(array, axes, split_axis=0, concat_axis=0, tiled=True)]
    all_to_all x8 -> x2, starting transfers between devices: 37.3 us -> 15 us  [exchange(): return lax.all_to_all(array, axes, split_axis=0, concat_axis=0, tiled=True)]
    unnamed x18 -> x6, local copies, waits for them, and re-layouts: 9.62 us -> 1.94 us
    pallas_call x3, Pallas kernels: 7.72 us -> 13.4 us  [the longest x1 8.12 us: project(): pl.pallas_call(project_kernel, grid=(steps,), in_specs=[whole((tokens, fe...]
    pallas_call x1, Pallas kernels: 2.49 us -> 6.81 us  [turn(): pl.pallas_call(turn_kernel, grid_spec=pltpu.PrefetchScalarGridSpec(num_sc...]
    pallas_call x2 -> x1, Pallas kernels: 2.93 us -> 3.99 us  [weight_grad(): pl.pallas_call(weight_kernel, out_shape=jax.ShapeDtypeStruct((feat, width...]
    pallas_call x2 -> x1, Pallas kernels: 22.8 us -> 23.6 us  [attend(): pl.pallas_call(functools.partial(attend_kernel, heads=heads), grid_spec=p...]
  transfers between devices with their start and end apart: 8 -> 2, of which waited for: 6 -> 2; matrix products, arithmetic and copies ran while one was open for 0% -> 0% of each run, Pallas kernels for 16% -> 4%
where the time goes in v2:
time: 171 us; the launch traced here: 170 us
  blocking collectives  80 us (47%)
  Pallas kernels  47.8 us (28%)
  waiting for transfers between devices  22.8 us (13%)
  starting transfers between devices  15 us (9%)
  between operations  1.96 us (1%)
  local copies, waits for them, and re-layouts  1.94 us (1%)
    all_to_all x3, blocking collectives, exchange(): return lax.all_to_all(array, axes, split_axis=0, concat_axis=0, tiled=True)  80 us
    pallas_call x1, Pallas kernels, attend(): pl.pallas_call(functools.partial(attend_kernel, heads=heads), grid_spec=p...  23.6 us
    all_to_all x2, waiting for transfers between devices, exchange(): return lax.all_to_all(array, axes, split_axis=0, concat_axis=0, tiled=True)  22.8 us
    all_to_all x2, starting transfers between devices, exchange(): return lax.all_to_all(array, axes, split_axis=0, concat_axis=0, tiled=True)  15 us
    pallas_call x1, Pallas kernels, project(): pl.pallas_call(project_kernel, grid=(steps,), in_specs=[whole((tokens, fe...  8.12 us
    pallas_call x1, Pallas kernels, turn(): pl.pallas_call(turn_kernel, grid_spec=pltpu.PrefetchScalarGridSpec(num_sc...  6.81 us
    pallas_call x1, Pallas kernels, weight_grad(): pl.pallas_call(weight_kernel, out_shape=jax.ShapeDtypeStruct((feat, width...  3.99 us
  transfers between devices with their start and end apart: 2, of which 2 were waited for; matrix products, arithmetic and copies ran while one was open for 0% of the time, Pallas kernels for 4%

profile of v2, /device:TPU:0, one launch (start us, length us, event | category | flops | bytes accessed | tf_op | source)
XLA Modules:
  0.0 170.2 jit_solution(18165960366851967612)
XLA Ops:
  0.6 8.1 %project.1 = (bf16[8,128,512]{2,1,0:T(8,128)(2,1)}, bf16[8,128,1024]{2,1,0:T(8,128)(2,1)}) custom-call(bf16[128,7680]{1,0:T(8,128)(2,1)} %bitcast.18, bf16[7680,256]{1,0:T(8,128)(2,1)} %wk_ref.1, bf16[7680,256]{1,0:T(8,128)(2,1)} %wv_ref.1, f32[1,128]{1,0:T(1,128)} %bitcast.22), custom_call_target="tpu_custom_call" | custom-call | flops 1006632960 | bytes 11796480 | tf_op jit(solution)/shard_map/project/pallas_call | solution.py:94
  8.8 11.5 %all-to-all-start = ((bf16[64,16,512]{2,1,0:T(8,128)(2,1)}), bf16[64,16,512]{2,1,0:T(8,128)(2,1)S(1)}, u32[]{:S(2)}, u32[]{:S(2)}) async-start(bf16[64,16,512]{2,1,0:T(8,128)(2,1)} %bitcast.20), calls=%async_computation | async-start | bytes 2097152 | tf_op jit(solution)/shard_map/all_to_all | solution.py:330
  21.6 0.7 pad_add_fusion.ctl_ref
  22.2 16.1 %all-to-all-done = bf16[64,16,512]{2,1,0:T(8,128)(2,1)S(1)} async-done(((bf16[64,16,512]{2,1,0:T(8,128)(2,1)}), bf16[64,16,512]{2,1,0:T(8,128)(2,1)S(1)}, u32[]{:S(2)}, u32[]{:S(2)}) %all-to-all-start) | async-done | bytes 1048608 | tf_op jit(solution)/shard_map/all_to_all | solution.py:330
  38.3 0.0 copy-start.2
  38.3 1.0 copy-done.2
  39.3 23.6 %attend.1 = (bf16[512,2048]{1,0:T(8,128)(2,1)}, bf16[512,2048]{1,0:T(8,128)(2,1)}, bf16[1024,512]{1,0:T(8,128)(2,1)}) custom-call(s32[4]{0:T(128)} %pad_add_fusion.ctl_ref, bf16[512,2048]{1,0:T(8,128)(2,1)} %bitcast.24, bf16[512,2048]{1,0:T(8,128)(2,1)} %bitcast.25, bf16[1024,512]{1,0:T(8,128)(2,1)} %bitcast.19), custom_call_target="tpu_custom_call" | custom-call | flops 25769803776 | bytes 8388608 | tf_op jit(solution)/shard_map/attend/pallas_call | solution.py:195
  62.9 0.0 copy-start.1
  62.9 18.3 %all_to_all.25.parts_ref = bf16[8,128,512]{2,1,0:T(8,128)(2,1)} all-to-all(bf16[8,128,512]{2,1,0:T(8,128)(2,1)} %bitcast.21), channel_id=1, replica_groups=mesh['dp'=8,'seq'=8,'mp'=2] {'seq'}, dimensions={0} | all-to-all | bytes 2097152 | tf_op jit(solution)/shard_map/all_to_all | solution.py:330
  81.2 0.0 copy-done.1
  81.2 44.4 %all_to_all.26 = bf16[8,128,1024]{2,1,0:T(8,128)(2,1)} all-to-all(bf16[8,128,1024]{2,1,0:T(8,128)(2,1)S(1)} %copy-done.1), channel_id=1, replica_groups=mesh['dp'=8,'seq'=8,'mp'=2] {'dp'}, dimensions={0} | all-to-all | bytes 4194304 | tf_op jit(solution)/shard_map/all_to_all | solution.py:330
  125.6 3.3 %norm_back.1 = bf16[8,128,512]{2,1,0:T(8,128)(2,1)} custom-call(s32[4]{0:T(128)} %pad_add_fusion.ctl_ref, bf16[8,128,512]{2,1,0:T(8,128)(2,1)} %all_to_all.25.parts_ref, bf16[8,8,16,1024]{3,2,1,0:T(8,128)(2,1)} %bitcast.14, f32[1,128]{1,0:T(1,128)} %bitcast.23), custom_call_target="tpu_custom_call" | custom-call | tf_op jit(solution)/shard_map/norm_back/pallas_call | solution.py:246
  128.9 3.6 %all-to-all-start.3 = ((bf16[8,128,512]{2,1,0:T(8,128)(2,1)}), bf16[8,128,512]{2,1,0:T(8,128)(2,1)S(1)}, u32[]{:S(2)}, u32[]{:S(2)}) async-start(bf16[8,128,512]{2,1,0:T(8,128)(2,1)} %norm_back.1), calls=%async_computation.3 | async-start | bytes 2097152 | tf_op jit(solution)/shard_map/all_to_all | solution.py:330
  132.4 6.8 %turn.1.f_ref = bf16[960,1024]{1,0:T(8,128)(2,1)} custom-call(s32[4]{0:T(128)} %pad_add_fusion.ctl_ref, bf16[8,8,16,1024]{3,2,1,0:T(8,128)(2,1)} %bitcast.15), custom_call_target="tpu_custom_call" | custom-call | tf_op jit(solution)/shard_map/turn/pallas_call | solution.py:283
  139.3 6.7 %all-to-all-done.3 = bf16[8,128,512]{2,1,0:T(8,128)(2,1)S(1)} async-done(((bf16[8,128,512]{2,1,0:T(8,128)(2,1)}), bf16[8,128,512]{2,1,0:T(8,128)(2,1)S(1)}, u32[]{:S(2)}, u32[]{:S(2)}) %all-to-all-start.3) | async-done | bytes 1048608 | tf_op jit(solution)/shard_map/all_to_all | solution.py:330
  145.9 0.0 copy-start
  145.9 1.0 copy-done
  146.9 4.0 %weight_grad.1 = bf16[960,512]{1,0:T(8,128)(2,1)} custom-call(bf16[960,1024]{1,0:T(8,128)(2,1)} %turn.1.f_ref, bf16[1024,512]{1,0:T(8,128)(2,1)} %bitcast.16), custom_call_target="tpu_custom_call" | custom-call | flops 1006632960 | bytes 1966080 | tf_op jit(solution)/shard_map/weight_grad/pallas_call | solution.py:304
  150.9 17.4 %all_to_all.27.parts_ref = bf16[8,120,512]{2,1,0:T(8,128)(2,1)} all-to-all(bf16[8,120,512]{2,1,0:T(8,128)(2,1)} %bitcast.17), channel_id=1, replica_groups=mesh['dp'=8,'seq'=8,'mp'=2] {'seq'}, dimensions={0} | all-to-all | bytes 1966080 | tf_op jit(solution)/shard_map/all_to_all | solution.py:330
  168.3 2.0 %finish.1 = (f32[120,256]{1,0:T(8,128)}, f32[120,256]{1,0:T(8,128)}) custom-call(bf16[8,120,512]{2,1,0:T(8,128)(2,1)} %all_to_all.27.parts_ref), custom_call_target="tpu_custom_call" | custom-call | tf_op jit(solution)/shard_map/finish/pallas_call | solution.py:326
Async XLA Ops:
  8.8 29.6 %all-to-all-start = ((bf16[64,16,512]{2,1,0:T(8,128)(2,1)}), bf16[64,16,512]{2,1,0:T(8,128)(2,1)S(1)}, u32[]{:S(2)}, u32[]{:S(2)}) async-start(bf16[64,16,512]{2,1,0:T(8,128)(2,1)} %bitcast.20), calls=%async_computation | async-start | bytes 2097152 | tf_op jit(solution)/shard_map/all_to_all | solution.py:330
  38.3 1.0 copy-start.2
  62.9 18.3 %copy-start.1 = (bf16[8,128,1024]{2,1,0:T(8,128)(2,1)S(1)}, bf16[8,128,1024]{2,1,0:T(8,128)(2,1)}, u32[]{:S(2)}) copy-start(bf16[8,128,1024]{2,1,0:T(8,128)(2,1)} %get-tuple-element.18) | copy-start | bytes 6291460
  128.9 17.1 %all-to-all-start.3 = ((bf16[8,128,512]{2,1,0:T(8,128)(2,1)}), bf16[8,128,512]{2,1,0:T(8,128)(2,1)S(1)}, u32[]{:S(2)}, u32[]{:S(2)}) async-start(bf16[8,128,512]{2,1,0:T(8,128)(2,1)} %norm_back.1), calls=%async_computation.3 | async-start | bytes 2097152 | tf_op jit(solution)/shard_map/all_to_all | solution.py:330
  145.9 1.0 copy-start

commit v3 on v2

v3 whole, which is shorter than its diff:
```python
import functools

import jax
import jax.numpy as jnp
from jax import lax
from jax.experimental import pallas as pl
from jax.experimental.pallas import tpu as pltpu
from jax.sharding import PartitionSpec as P

HEAD_DIM = 128
TILES = 4
EPSILON = 1e-05
SCALE = HEAD_DIM**-0.5
EXP2_SCALE = SCALE * 1.4426950408889634
BF16 = jnp.bfloat16
F32 = jnp.float32
LANES = 128
SUBLANES = 8
CHUNK = 128
VMEM_LIMIT = 59 * 2**20
SMALL_LIMIT = 16 * 2**20

NN = (((1,), (0,)), ((), ()))
NT = (((1,), (1,)), ((), ()))


def whole(shape):
    return pl.BlockSpec(shape, lambda *_: (0,) * len(shape))


def params(axes, limit=VMEM_LIMIT):
    return pltpu.CompilerParams(
        vmem_limit_bytes=limit, dimension_semantics=("arbitrary",) * axes
    )


def project_kernel(f_ref, wk_ref, wv_ref, gain_ref, send_ref, pre_ref, total):
    step, steps = pl.program_id(0), pl.num_programs(0)
    kv_dim = wk_ref.shape[1]

    @pl.when(step == 0)
    def _():
        total[...] = jnp.zeros_like(total)

    total[:, :kv_dim] += jnp.dot(f_ref[...], wk_ref[...], preferred_element_type=F32)
    total[:, kv_dim:] += jnp.dot(f_ref[...], wv_ref[...], preferred_element_type=F32)

    @pl.when(step == steps - 1)
    def _():
        pre_ref[...] = total[:, :kv_dim]
        for group in range(kv_dim // HEAD_DIM):
            cols = slice(group * HEAD_DIM, (group + 1) * HEAD_DIM)
            head = total[:, cols]
            factor = lax.rsqrt(jnp.mean(head * head, axis=-1, keepdims=True) + EPSILON)
            key = (head * factor * gain_ref[...]).astype(BF16)
            start = kv_dim + group * HEAD_DIM
            value = total[:, start : start + HEAD_DIM].astype(BF16)
            at = 2 * group * HEAD_DIM
            for copy in range(send_ref.shape[0]):
                send_ref[copy, :, at : at + HEAD_DIM] = key
                send_ref[copy, :, at + HEAD_DIM : at + 2 * HEAD_DIM] = value


def project(feats, w_key, w_value, gain, copies):
    tokens, feat = feats.shape
    kv_dim = w_key.shape[1]
    steps = 5
    depth = feat // steps
    send, pre = (copies, tokens, 2 * kv_dim), (tokens, kv_dim)
    return pl.pallas_call(
        project_kernel,
        grid=(steps,),
        in_specs=[
            pl.BlockSpec((tokens, depth), lambda k: (0, k)),
            pl.BlockSpec((depth, kv_dim), lambda k: (k, 0)),
            pl.BlockSpec((depth, kv_dim), lambda k: (k, 0)),
            whole((1, HEAD_DIM)),
        ],
        out_specs=[whole(send), whole(pre)],
        out_shape=[jax.ShapeDtypeStruct(send, BF16), jax.ShapeDtypeStruct(pre, F32)],
        scratch_shapes=[pltpu.VMEM((tokens, 2 * kv_dim), F32)],
        compiler_params=params(1),
        cost_estimate=pl.CostEstimate(
            flops=4 * tokens * feat * kv_dim,
            bytes_accessed=4 * feat * kv_dim + 4 * tokens * feat,
            transcendentals=0,
        ),
        name="project",
    )(feats, w_key, w_value, gain)


def cut_kernel(f_ref, pre_ref, win_ref):
    windows, tokens, width = win_ref.shape
    tiles = f_ref.shape[1] // LANES
    own = tokens // windows
    half = LANES // 2
    lane = lax.broadcasted_iota(jnp.int32, (own, LANES), 1)
    for window in range(windows):
        tile = window * tiles // windows
        win_ref[window] = f_ref[:, tile * LANES : tile * LANES + width]
        head = pre_ref[window * own : (window + 1) * own]
        high = head.astype(BF16).astype(F32)
        pair = jnp.concatenate([high, head - high], axis=1)
        place = 1 - window % 2
        at = (width - LANES) * place
        for block in range(windows):
            piece = pair[:, block // 2 * LANES : (block // 2 + 1) * LANES]
            if block % 2 != place:
                piece = pltpu.roll(piece, half, axis=1)
            rows = slice(block * own, (block + 1) * own)
            kept = win_ref[window, rows, at : at + LANES].astype(F32)
            mixed = jnp.where((lane >= half) == bool(place), piece, kept)
            win_ref[window, rows, at : at + LANES] = mixed.astype(BF16)


def cut(feats, key_pre, windows):
    tokens, feat = feats.shape
    width = -(-(feat // windows) // LANES) * LANES
    return pl.pallas_call(
        cut_kernel,
        out_shape=jax.ShapeDtypeStruct((windows, tokens, width), BF16),
        compiler_params=params(0, SMALL_LIMIT),
        cost_estimate=pl.CostEstimate(
            flops=0, bytes_accessed=6 * tokens * feat, transcendentals=0
        ),
        name="cut",
    )(feats, key_pre)


def attend_kernel(
    ctl_ref, q_ref, d_ref, kv_ref, prob_ref, grad_ref, dkv_ref, dk_sum, dv_sum, powers_ref, live_ref, *, heads
):
    step, steps = pl.program_id(1), pl.num_programs(1)
    rows = q_ref.shape[0]
    img = kv_ref.shape[0]

    @pl.when(step == 0)
    def _():
        dk_sum[...] = jnp.zeros_like(dk_sum)
        dv_sum[...] = jnp.zeros_like(dv_sum)

    def run(length):
        position = ctl_ref[1] + lax.broadcasted_iota(jnp.int32, (rows, HEAD_DIM), 0)
        live = position >= ctl_ref[2]
        chunks = [slice(at, at + CHUNK) for at in range(0, length, CHUNK)]
        folded = (CHUNK // SUBLANES, SUBLANES, rows)

        def against(chunk, start, other):
            left = kv_ref[chunk, start : start + HEAD_DIM]
            out = lax.dot_general(left, other, NT, preferred_element_type=F32)
            return out.reshape(folded)

        def first(head):
            cols = slice(head * HEAD_DIM, (head + 1) * HEAD_DIM)
            here = slice(head * rows, (head + 1) * rows)
            query = q_ref[:, cols]
            cotangent = jnp.where(live, d_ref[:, cols], jnp.zeros((), BF16))
            live_ref[here] = cotangent
            tops, sums, deltas = [], [], []
            for chunk in chunks:
                scores = against(chunk, 0, query)
                top = jnp.max(scores, axis=0)
                powers = jnp.exp2((scores - top[None]) * EXP2_SCALE)
                powers_ref[chunk, here] = powers.reshape(CHUNK, rows)
                tops.append(top)
                sums.append(jnp.sum(powers, axis=0))
                deltas.append(jnp.sum(powers * against(chunk, HEAD_DIM, cotangent), axis=0))
            row_max = jnp.max(functools.reduce(jnp.maximum, tops), axis=0, keepdims=True)
            factors = [jnp.exp2((top - row_max) * EXP2_SCALE) for top in tops]

            def over_rows(parts):
                total = sum(part * factor for part, factor in zip(parts, factors))
                return jnp.sum(total, axis=0, keepdims=True)

            inverse = 1.0 / over_rows(sums)
            delta = over_rows(deltas) * inverse
            return cotangent, here, [factor * inverse for factor in factors], delta

        def second(cotangent, here, factors, delta):
            for chunk, factor in zip(chunks, factors):
                prob = powers_ref[chunk, here].reshape(folded) * factor[None]
                prob_ref[chunk, here] = prob.reshape(CHUNK, rows).astype(BF16)
                score_grad = prob * (against(chunk, HEAD_DIM, cotangent) - delta[None])
                grad_ref[chunk, here] = score_grad.reshape(CHUNK, rows).astype(BF16)

        held = first(0)
        for head in range(heads):
            ahead = first(head + 1) if head + 1 < heads else None
            second(*held)
            held = ahead
        queries = jnp.concatenate(
            [q_ref[:, head * HEAD_DIM : (head + 1) * HEAD_DIM] for head in range(heads)], axis=0
        )
        dk_sum[:length] += jnp.dot(grad_ref[:length], queries, preferred_element_type=F32)
        dv_sum[:length] += jnp.dot(prob_ref[:length], live_ref[...], preferred_element_type=F32)

    for count in range(1, TILES + 1):
        pl.when(ctl_ref[0] == count)(functools.partial(run, count * (img // TILES)))

    @pl.when(step == steps - 1)
    def _():
        dkv_ref[:, :HEAD_DIM] = (dk_sum[...] * SCALE).astype(BF16)
        dkv_ref[:, HEAD_DIM:] = dv_sum[...].astype(BF16)


def attend(ctl, queries, out_grad, keys_values):
    rows, width = queries.shape
    img, pairs = keys_values.shape
    groups = pairs // (2 * HEAD_DIM)
    heads = 2
    steps = width // groups // HEAD_DIM // heads
    cols = pl.BlockSpec((rows, heads * HEAD_DIM), lambda g, h, ctl: (0, g * steps + h))
    pair = pl.BlockSpec((img, 2 * HEAD_DIM), lambda g, h, ctl: (0, g))
    square = pl.BlockSpec((img, heads * rows), lambda g, h, ctl: (0, g * steps + h))
    big = jax.ShapeDtypeStruct((img, width // HEAD_DIM * rows), BF16)
    return pl.pallas_call(
        functools.partial(attend_kernel, heads=heads),
        grid_spec=pltpu.PrefetchScalarGridSpec(
            num_scalar_prefetch=1,
            grid=(groups, steps),
            in_specs=[cols, cols, pair],
            out_specs=[square, square, pair],
            scratch_shapes=[pltpu.VMEM((img, HEAD_DIM), F32)] * 2
            + [
                pltpu.VMEM((img, heads * rows), F32),
                pltpu.VMEM((heads * rows, HEAD_DIM), BF16),
            ],
        ),
        out_shape=[big, big, jax.ShapeDtypeStruct((img, pairs), BF16)],
        compiler_params=params(2),
        cost_estimate=pl.CostEstimate(
            flops=20 * rows * width * img, bytes_accessed=8 * rows * width, transcendentals=0
        ),
        name="attend",
    )(ctl, queries, out_grad, keys_values)


def apply_kernel(ctl_ref, left_ref, kv_ref, out_ref, turned_ref, *, heads, start, masked):
    rows = out_ref.shape[0]
    img = kv_ref.shape[0]

    @pl.when(pl.program_id(1) == 0)
    def _():
        turned_ref[...] = kv_ref[:, start : start + HEAD_DIM].T

    def run(length):
        position = ctl_ref[1] + lax.broadcasted_iota(jnp.int32, (rows, HEAD_DIM), 0)
        live = position >= ctl_ref[2]
        for head in range(heads):
            left = left_ref[:length, head * rows : (head + 1) * rows]
            out = jnp.dot(turned_ref[:, :length], left, preferred_element_type=F32).T
            out = jnp.where(live, out, 0.0) if masked else out * SCALE
            out_ref[:, head * HEAD_DIM : (head + 1) * HEAD_DIM] = out.astype(BF16)

    for count in range(1, TILES + 1):
        pl.when(ctl_ref[0] == count)(functools.partial(run, count * (img // TILES)))


def apply(ctl, left, keys_values, rows, start, masked, name):
    img, pairs = keys_values.shape
    groups = pairs // (2 * HEAD_DIM)
    heads = 2
    all_heads = left.shape[1] // rows
    steps = all_heads // groups // heads
    return pl.pallas_call(
        functools.partial(apply_kernel, heads=heads, start=start, masked=masked),
        grid_spec=pltpu.PrefetchScalarGridSpec(
            num_scalar_prefetch=1,
            grid=(groups, steps),
            in_specs=[
                pl.BlockSpec((img, heads * rows), lambda g, h, ctl: (0, g * steps + h)),
                pl.BlockSpec((img, 2 * HEAD_DIM), lambda g, h, ctl: (0, g)),
            ],
            out_specs=pl.BlockSpec((rows, heads * HEAD_DIM), lambda g, h, ctl: (0, g * steps + h)),
            scratch_shapes=[pltpu.VMEM((HEAD_DIM, img), BF16)],
        ),
        out_shape=jax.ShapeDtypeStruct((rows, all_heads * HEAD_DIM), BF16),
        compiler_params=params(2),
        cost_estimate=pl.CostEstimate(
            flops=2 * img * rows * all_heads * HEAD_DIM,
            bytes_accessed=2 * img * rows * all_heads,
            transcendentals=0,
        ),
        name=name,
    )(ctl, left, keys_values)


def norm_back_kernel(ctl_ref, parts_ref, pre_ref, gain_ref, out_ref):
    grad = jnp.sum(parts_ref[...].astype(F32), axis=0)
    tokens, width = grad.shape
    place = 1 - ctl_ref[3]
    half = LANES // 2
    lane = lax.broadcasted_iota(jnp.int32, (tokens, LANES), 1)
    blocks = pre_ref.shape[1] // 2

    def piece(block):
        high = pre_ref[:, block].astype(F32).reshape(tokens, LANES)
        low = pre_ref[:, blocks + block].astype(F32).reshape(tokens, LANES)
        held = high + low
        return jnp.where(place == block % 2, held, pltpu.roll(held, half, axis=1))

    for group in range(width // (2 * HEAD_DIM)):
        head = jnp.where(lane < half, piece(2 * group), piece(2 * group + 1))
        at = 2 * group * HEAD_DIM
        key_grad = grad[:, at : at + HEAD_DIM]
        factor = lax.rsqrt(jnp.mean(head * head, axis=-1, keepdims=True) + EPSILON)
        gained = gain_ref[...] * key_grad
        inner = jnp.mean(head * gained, axis=-1, keepdims=True)
        pre_grad = (factor * gained - factor * factor * factor * head * inner).astype(BF16)
        value_grad = grad[:, at + HEAD_DIM : at + 2 * HEAD_DIM].astype(BF16)
        for copy in range(out_ref.shape[0]):
            out_ref[copy, :, at : at + HEAD_DIM] = pre_grad
            out_ref[copy, :, at + HEAD_DIM : at + 2 * HEAD_DIM] = value_grad


def norm_back(ctl, parts, windows, gain, copies):
    tokens, width = parts.shape[1:]
    sources, rows, own, lanes = windows.shape
    last = lanes // LANES - 1
    return pl.pallas_call(
        norm_back_kernel,
        grid_spec=pltpu.PrefetchScalarGridSpec(
            num_scalar_prefetch=1,
            grid=(1,),
            in_specs=[
                whole(parts.shape),
                pl.BlockSpec(
                    (sources, rows, own, LANES), lambda i, ctl: (0, 0, 0, last * (1 - ctl[3]))
                ),
                whole(gain.shape),
            ],
            out_specs=whole((copies, tokens, width)),
        ),
        out_shape=jax.ShapeDtypeStruct((copies, tokens, width), BF16),
        compiler_params=params(1, SMALL_LIMIT),
        name="norm_back",
    )(ctl, parts, windows, gain)


def turn_kernel(ctl_ref, f_ref, out_ref):
    odd = ctl_ref[3]
    turned = f_ref[...].reshape(-1, f_ref.shape[-1]).T
    rows = out_ref.shape[0]
    spare = turned.shape[0] - rows

    @pl.when(odd == 0)
    def _():
        out_ref[...] = turned[:rows]

    @pl.when(odd != 0)
    def _():
        out_ref[...] = turned[spare:]


def turn(ctl, windows, feat):
    sources, rows, own, width = windows.shape
    tokens = sources * own
    return pl.pallas_call(
        turn_kernel,
        grid_spec=pltpu.PrefetchScalarGridSpec(
            num_scalar_prefetch=1,
            grid=(rows,),
            in_specs=[pl.BlockSpec((sources, 1, own, width), lambda r, ctl: (0, r, 0, 0))],
            out_specs=pl.BlockSpec((feat, tokens), lambda r, ctl: (0, r)),
        ),
        out_shape=jax.ShapeDtypeStruct((feat, rows * tokens), BF16),
        compiler_params=params(1, SMALL_LIMIT),
        name="turn",
    )(ctl, windows)


def weight_kernel(f_ref, g_ref, out_ref):
    out_ref[...] = jnp.dot(f_ref[...], g_ref[...], preferred_element_type=F32).astype(BF16)


def weight_grad(turned, grads):
    feat, tokens = turned.shape
    width = grads.shape[1]
    return pl.pallas_call(
        weight_kernel,
        out_shape=jax.ShapeDtypeStruct((feat, width), BF16),
        compiler_params=params(0, SMALL_LIMIT),
        cost_estimate=pl.CostEstimate(
            flops=2 * feat * tokens * width, bytes_accessed=2 * feat * tokens, transcendentals=0
        ),
        name="weight_grad",
    )(turned, grads)


def finish_kernel(parts_ref, key_ref, value_ref):
    total = jnp.sum(parts_ref[...].astype(F32), axis=0)
    for group in range(total.shape[1] // (2 * HEAD_DIM)):
        cols = slice(group * HEAD_DIM, (group + 1) * HEAD_DIM)
        at = 2 * group * HEAD_DIM
        key_ref[:, cols] = total[:, at : at + HEAD_DIM]
        value_ref[:, cols] = total[:, at + HEAD_DIM : at + 2 * HEAD_DIM]


def finish(parts):
    out = jax.ShapeDtypeStruct((parts.shape[1], parts.shape[2] // 2), F32)
    return pl.pallas_call(
        finish_kernel,
        out_shape=[out, out],
        compiler_params=params(0, SMALL_LIMIT),
        name="finish",
    )(parts)


def exchange(array, axes):
    return lax.all_to_all(array, axes, split_axis=0, concat_axis=0, tiled=True)


def on_device(queries, features, w_key, w_value, key_gain, out_grad, tile_counts, text_start):
    dp, seq = lax.axis_size("dp"), lax.axis_size("seq")
    rows, own, feat = features.shape
    text_dev = queries.shape[1]
    pairs = 2 * w_key.shape[1]
    tokens = rows * own
    gain = key_gain.reshape(1, HEAD_DIM)
    dp_index, seq_index = lax.axis_index("dp"), lax.axis_index("seq")
    ctl = jnp.stack([tile_counts[0], seq_index * text_dev, text_start[0], dp_index & 1])
    feats = features.reshape(tokens, feat)
    send, key_pre = project(feats, w_key, w_value, gain, seq)
    windows = cut(feats, key_pre, dp)
    arrived = exchange(send.reshape(seq * dp, own, pairs), ("seq", "dp"))
    windows, arrived, ctl = lax.optimization_barrier((windows, arrived, ctl))
    keys_values = arrived.reshape(seq * tokens, pairs)
    windows = exchange(windows, "dp").reshape(dp, rows, own, -1)
    probs, score_grads, grads = attend(ctl, queries[0], out_grad[0], keys_values)
    grads, windows = lax.optimization_barrier((grads, windows))
    shares = exchange(grads.reshape(seq, tokens, pairs), "seq")
    attended = apply(ctl, probs, keys_values, text_dev, HEAD_DIM, True, "attended")
    shares, attended = lax.optimization_barrier((shares, attended))
    rounded = norm_back(ctl, shares, windows, gain, dp)
    everywhere = exchange(rounded, "dp").reshape(dp * tokens, pairs)
    turned = turn(ctl, windows, feat // dp)
    query_grad = apply(ctl, score_grads, keys_values, text_dev, 0, False, "query_grad")
    everywhere, query_grad = lax.optimization_barrier((everywhere, query_grad))
    partial = weight_grad(turned, everywhere)
    pieces = exchange(partial.reshape(seq, feat // dp // seq, pairs), "seq")
    key_weight, value_weight = finish(pieces)
    return attended[None], query_grad[None], key_weight, value_weight


def solution(mesh):
    placed = (
        P("dp", "seq", "mp"),
        P(None, ("seq", "dp"), None),
        P(None, "mp"),
        P(None, "mp"),
        P(),
        P("dp", "seq", "mp"),
        P("dp"),
        P("dp"),
    )
    return jax.shard_map(
        on_device,
        mesh=mesh,
        in_specs=placed,
        out_specs=(
            P("dp", "seq", "mp"),
            P("dp", "seq", "mp"),
            P(("dp", "seq"), "mp"),
            P(("dp", "seq"), "mp"),
        ),
        check_vma=False,
    )
```

time: 171 us -> 138 us (0.81)
  blocking collectives: 80 us -> 17.5 us
  starting transfers between devices: 15 us -> 28.6 us
  waiting for transfers between devices: 22.8 us -> 32.1 us
  Pallas kernels: 47.8 us -> 51.9 us
  local copies, waits for them, and re-layouts: 1.94 us -> 4.17 us
    all_to_all x3 -> x1, blocking collectives: 80 us -> 17.5 us  [exchange(): return lax.all_to_all(array, axes, split_axis=0, concat_axis=0, tiled=True)]
    pallas_call x2 -> x5, Pallas kernels: 10.1 us -> 30.4 us  [the longest x2 22.4 us: apply(): pl.pallas_call(functools.partial(apply_kernel, heads=heads, start=start,...]
    all_to_all x2 -> x4, starting transfers between devices: 15 us -> 28.6 us  [exchange(): return lax.all_to_all(array, axes, split_axis=0, concat_axis=0, tiled=True)]
    all_to_all x2 -> x4, waiting for transfers between devices: 22.8 us -> 32.1 us  [exchange(): return lax.all_to_all(array, axes, split_axis=0, concat_axis=0, tiled=True)]
    pallas_call x1, Pallas kernels: 23.6 us -> 15.8 us  [attend(): pl.pallas_call(functools.partial(attend_kernel, heads=heads), grid_spec=p...]
    pallas_call x1, Pallas kernels: 6.81 us -> 2.49 us  [turn(): pl.pallas_call(turn_kernel, grid_spec=pltpu.PrefetchScalarGridSpec(num_sc...]
    pallas_call x1, Pallas kernels: 3.99 us -> 1.17 us  [weight_grad(): pl.pallas_call(weight_kernel, out_shape=jax.ShapeDtypeStruct((feat, width...]
    unnamed x6 -> x18, local copies, waits for them, and re-layouts: 1.94 us -> 4.17 us
  transfers between devices with their start and end apart: 2 -> 4, of which waited for: 2 -> 4; matrix products, arithmetic and copies ran while one was open for 0% -> 0% of each run, Pallas kernels for 4% -> 30%
where the time goes in v3:
time: 138 us; the launch traced here: 137 us
  Pallas kernels  51.9 us (38%)
  waiting for transfers between devices  32.1 us (23%)
  starting transfers between devices  28.6 us (21%)
  blocking collectives  17.5 us (13%)
  local copies, waits for them, and re-layouts  4.17 us (3%)
  between operations  2.04 us (1%)
    all_to_all x4, waiting for transfers between devices, exchange(): return lax.all_to_all(array, axes, split_axis=0, concat_axis=0, tiled=True)  32.1 us
    all_to_all x4, starting transfers between devices, exchange(): return lax.all_to_all(array, axes, split_axis=0, concat_axis=0, tiled=True)  28.6 us
    pallas_call x2, Pallas kernels, apply(): pl.pallas_call(functools.partial(apply_kernel, heads=heads, start=start,...  22.4 us
    all_to_all x1, blocking collectives, exchange(): return lax.all_to_all(array, axes, split_axis=0, concat_axis=0, tiled=True)  17.5 us
    pallas_call x1, Pallas kernels, attend(): pl.pallas_call(functools.partial(attend_kernel, heads=heads), grid_spec=p...  15.8 us
    pallas_call x1, Pallas kernels, project(): pl.pallas_call(project_kernel, grid=(steps,), in_specs=[pl.BlockSpec((tok...  6.97 us
    unnamed x18, local copies, waits for them, and re-layouts  4.17 us
  transfers between devices with their start and end apart: 4, of which 4 were waited for; matrix products, arithmetic and copies ran while one was open for 0% of the time, Pallas kernels for 30%

profile of v3, /device:TPU:0, one launch (start us, length us, event | category | flops | bytes accessed | tf_op | source)
XLA Modules:
  0.0 137.0 jit_solution(5320319045157262993)
XLA Ops:
  0.6 7.0 %project.1 = (bf16[8,128,512]{2,1,0:T(8,128)(2,1)}, f32[128,256]{1,0:T(8,128)}) custom-call(bf16[128,7680]{1,0:T(8,128)(2,1)} %bitcast.16, bf16[7680,256]{1,0:T(8,128)(2,1)} %wk_ref.1, bf16[7680,256]{1,0:T(8,128)(2,1)} %wv_ref.1, f32[1,128]{1,0:T(1,128)} %bitcast.20), custom_call_target="tpu_custom_call" | custom-call | flops 1006632960 | bytes 11796480 | tf_op jit(solution)/shard_map/project/pallas_call | solution.py:70
  7.6 0.0 copy-start.1
  7.6 0.0 copy-start.4
  7.6 11.6 %all-to-all-start = ((bf16[64,16,512]{2,1,0:T(8,128)(2,1)}), bf16[64,16,512]{2,1,0:T(8,128)(2,1)S(1)}, u32[]{:S(2)}, u32[]{:S(2)}) async-start(bf16[64,16,512]{2,1,0:T(8,128)(2,1)} %bitcast.27), calls=%async_computation | async-start | bytes 2097152 | tf_op jit(solution)/shard_map/all_to_all | solution.py:410
  19.3 0.0 copy-done.1
  19.3 0.0 copy-done.4
  19.3 0.2 cut.1
  19.5 0.0 copy-start
  19.5 1.3 copy-done
  22.1 0.7 pad_add_fusion.ctl_ref
  22.8 14.5 %all-to-all-done = bf16[64,16,512]{2,1,0:T(8,128)(2,1)S(1)} async-done(((bf16[64,16,512]{2,1,0:T(8,128)(2,1)}), bf16[64,16,512]{2,1,0:T(8,128)(2,1)S(1)}, u32[]{:S(2)}, u32[]{:S(2)}) %all-to-all-start) | async-done | bytes 1048608 | tf_op jit(solution)/shard_map/all_to_all | solution.py:410
  37.3 0.0 copy-start.8
  37.3 3.8 %all-to-all-start.1 = ((bf16[8,128,1024]{2,1,0:T(8,128)(2,1)}), bf16[8,128,1024]{2,1,0:T(8,128)(2,1)S(1)}, u32[]{:S(2)}, u32[]{:S(2)}) async-start(bf16[8,128,1024]{2,1,0:T(8,128)(2,1)} %copy-done), calls=%async_computation.1 | async-start | bytes 4194304 | tf_op jit(solution)/shard_map/all_to_all | solution.py:410
  41.2 0.0 copy-done.8
  41.2 15.8 %attend.1 = (bf16[1024,8192]{1,0:T(8,128)(2,1)}, bf16[1024,8192]{1,0:T(8,128)(2,1)}, bf16[1024,512]{1,0:T(8,128)(2,1)}) custom-call(s32[4]{0:T(128)} %pad_add_fusion.ctl_ref, bf16[512,2048]{1,0:T(8,128)(2,1)} %bitcast.29, bf16[512,2048]{1,0:T(8,128)(2,1)} %bitcast.30, bf16[1024,512]{1,0:T(8,128)(2,1)} %bitcast.22), custom_call_target="tpu_custom_call" | custom-call | flops 21474836480 | bytes 8388608 | tf_op jit(solution)/shard_map/attend/pallas_call | solution.py:216
  57.0 11.3 %all-to-all-done.1 = bf16[8,128,1024]{2,1,0:T(8,128)(2,1)S(1)} async-done(((bf16[8,128,1024]{2,1,0:T(8,128)(2,1)}), bf16[8,128,1024]{2,1,0:T(8,128)(2,1)S(1)}, u32[]{:S(2)}, u32[]{:S(2)}) %all-to-all-start.1) | async-done | bytes 2097184 | tf_op jit(solution)/shard_map/all_to_all | solution.py:410
  68.3 3.7 %all-to-all-start.2 = ((bf16[8,128,512]{2,1,0:T(8,128)(2,1)}), bf16[8,128,512]{2,1,0:T(8,128)(2,1)S(1)}, u32[]{:S(2)}, u32[]{:S(2)}) async-start(bf16[8,128,512]{2,1,0:T(8,128)(2,1)} %bitcast.28), calls=%async_computation.2 | async-start | bytes 2097152 | tf_op jit(solution)/shard_map/all_to_all | solution.py:410
  72.0 0.0 copy-start.5
  72.0 0.0 copy-start.7
  72.0 11.1 %attended.1 = bf16[512,2048]{1,0:T(8,128)(2,1)} custom-call(s32[4]{0:T(128)} %pad_add_fusion.ctl_ref, bf16[1024,8192]{1,0:T(8,128)(2,1)} %get-tuple-element.27.left_ref, bf16[1024,512]{1,0:T(8,128)(2,1)} %bitcast.23), custom_call_target="tpu_custom_call" | custom-call | flops 2147483648 | bytes 16777216 | tf_op jit(solution)/shard_map/attended/pallas_call | solution.py:265
  83.2 4.4 %all-to-all-done.2.parts_ref = bf16[8,128,512]{2,1,0:T(8,128)(2,1)S(1)} async-done(((bf16[8,128,512]{2,1,0:T(8,128)(2,1)}), bf16[8,128,512]{2,1,0:T(8,128)(2,1)S(1)}, u32[]{:S(2)}, u32[]{:S(2)}) %all-to-all-start.2) | async-done | bytes 1048608 | tf_op jit(solution)/shard_map/all_to_all | solution.py:410
  87.6 0.0 copy-done.5
  87.6 0.0 copy-done.7
  87.6 2.0 %norm_back.1 = bf16[8,128,512]{2,1,0:T(8,128)(2,1)} custom-call(s32[4]{0:T(128)S(1)} %copy-done.5, bf16[8,128,512]{2,1,0:T(8,128)(2,1)S(1)} %all-to-all-done.2.parts_ref, bf16[8,8,16,1024]{3,2,1,0:T(8,128)(2,1)S(1)} %bitcast.14, f32[1,128]{1,0:T(1,128)S(1)} %bitcast.21), custom_call_target="tpu_custom_call" | custom-call | tf_op jit(solution)/shard_map/norm_back/pallas_call | solution.py:320
  89.6 9.4 %all-to-all-start.3 = ((bf16[8,128,512]{2,1,0:T(8,128)(2,1)}), bf16[8,128,512]{2,1,0:T(8,128)(2,1)S(1)}, u32[]{:S(2)}, u32[]{:S(2)}) async-start(bf16[8,128,512]{2,1,0:T(8,128)(2,1)} %norm_back.1), calls=%async_computation.3 | async-start | bytes 2097152 | tf_op jit(solution)/shard_map/all_to_all | solution.py:410
  98.9 0.0 copy-start.6
  98.9 11.3 %query_grad.1 = bf16[512,2048]{1,0:T(8,128)(2,1)} custom-call(s32[4]{0:T(128)} %pad_add_fusion.ctl_ref, bf16[1024,8192]{1,0:T(8,128)(2,1)} %get-tuple-element.31.left_ref, bf16[1024,512]{1,0:T(8,128)(2,1)} %bitcast.24), custom_call_target="tpu_custom_call" | custom-call | flops 2147483648 | bytes 16777216 | tf_op jit(solution)/shard_map/query_grad/pallas_call | solution.py:265
  110.2 0.0 copy-done.6
  110.2 2.5 %turn.1.f_ref = bf16[960,1024]{1,0:T(8,128)(2,1)S(1)} custom-call(s32[4]{0:T(128)S(1)} %copy-done.6, bf16[8,8,16,1024]{3,2,1,0:T(8,128)(2,1)S(1)} %bitcast.15), custom_call_target="tpu_custom_call" | custom-call | tf_op jit(solution)/shard_map/turn/pallas_call | solution.py:358
  112.7 0.0 copy-start.2
  112.7 1.3 copy-done.2
  114.0 1.9 %all-to-all-done.3 = bf16[8,128,512]{2,1,0:T(8,128)(2,1)S(1)} async-done(((bf16[8,128,512]{2,1,0:T(8,128)(2,1)}), bf16[8,128,512]{2,1,0:T(8,128)(2,1)S(1)}, u32[]{:S(2)}, u32[]{:S(2)}) %all-to-all-start.3) | async-done | bytes 1048608 | tf_op jit(solution)/shard_map/all_to_all | solution.py:410
  115.9 0.0 copy-start.3
  115.9 1.5 %copy-done.3 = bf16[960,1024]{1,0:T(8,128)(2,1)S(1)} copy-done((bf16[960,1024]{1,0:T(8,128)(2,1)S(1)}, bf16[960,1024]{1,0:T(8,128)(2,1)}, u32[]{:S(2)}) %copy-start.3) | copy-done | bytes 1966104
  117.5 1.2 weight_grad.1
  118.7 17.5 %all_to_all.25.parts_ref = bf16[8,120,512]{2,1,0:T(8,128)(2,1)S(1)} all-to-all(bf16[8,120,512]{2,1,0:T(8,128)(2,1)S(1)} %bitcast.19), channel_id=1, replica_groups=mesh['dp'=8,'seq'=8,'mp'=2] {'seq'}, dimensions={0} | all-to-all | bytes 1966080 | tf_op jit(solution)/shard_map/all_to_all | solution.py:410
  136.2 0.8 finish.1
Async XLA Ops:
  7.6 11.7 %copy-start.1 = (bf16[8,16,7680]{2,1,0:T(8,128)(2,1)S(1)}, bf16[8,16,7680]{2,1,0:T(8,128)(2,1)}, u32[]{:S(2)}) copy-start(bf16[8,16,7680]{2,1,0:T(8,128)(2,1)} %param.9) | copy-start | bytes 5898244
  7.6 11.7 %copy-start.4 = (f32[128,256]{1,0:T(8,128)S(1)}, f32[128,256]{1,0:T(8,128)}, u32[]{:S(2)}) copy-start(f32[128,256]{1,0:T(8,128)} %get-tuple-element.20.pre_ref) | copy-start | bytes 393220
  7.6 29.7 %all-to-all-start = ((bf16[64,16,512]{2,1,0:T(8,128)(2,1)}), bf16[64,16,512]{2,1,0:T(8,128)(2,1)S(1)}, u32[]{:S(2)}, u32[]{:S(2)}) async-start(bf16[64,16,512]{2,1,0:T(8,128)(2,1)} %bitcast.27), calls=%async_computation | async-start | bytes 2097152 | tf_op jit(solution)/shard_map/all_to_all | solution.py:410
  19.5 1.3 copy-start
  37.3 3.9 %copy-start.8 = (bf16[64,16,512]{2,1,0:T(8,128)(2,1)}, bf16[64,16,512]{2,1,0:T(8,128)(2,1)S(1)}, u32[]{:S(2)}) copy-start(bf16[64,16,512]{2,1,0:T(8,128)(2,1)S(1)} %all-to-all-done) | copy-start | bytes 3145732
  37.3 30.9 %all-to-all-start.1 = ((bf16[8,128,1024]{2,1,0:T(8,128)(2,1)}), bf16[8,128,1024]{2,1,0:T(8,128)(2,1)S(1)}, u32[]{:S(2)}, u32[]{:S(2)}) async-start(bf16[8,128,1024]{2,1,0:T(8,128)(2,1)} %copy-done), calls=%async_computation.1 | async-start | bytes 4194304 | tf_op jit(solution)/shard_map/all_to_all | solution.py:410
  68.3 19.3 %all-to-all-start.2 = ((bf16[8,128,512]{2,1,0:T(8,128)(2,1)}), bf16[8,128,512]{2,1,0:T(8,128)(2,1)S(1)}, u32[]{:S(2)}, u32[]{:S(2)}) async-start(bf16[8,128,512]{2,1,0:T(8,128)(2,1)} %bitcast.28), calls=%async_computation.2 | async-start | bytes 2097152 | tf_op jit(solution)/shard_map/all_to_all | solution.py:410
  72.0 15.6 %copy-start.5 = (s32[4]{0:T(128)S(1)}, s32[4]{0:T(128)}, u32[]{:S(2)}) copy-start(s32[4]{0:T(128)} %pad_add_fusion.ctl_ref) | copy-start | bytes 52
  72.0 15.6 %copy-start.7 = (f32[128]{0:T(128)S(1)}, f32[128]{0:T(128)}, u32[]{:S(2)}) copy-start(f32[128]{0:T(128)} %param.12) | copy-start | bytes 1540
  89.6 26.4 %all-to-all-start.3 = ((bf16[8,128,512]{2,1,0:T(8,128)(2,1)}), bf16[8,128,512]{2,1,0:T(8,128)(2,1)S(1)}, u32[]{:S(2)}, u32[]{:S(2)}) async-start(bf16[8,128,512]{2,1,0:T(8,128)(2,1)} %norm_back.1), calls=%async_computation.3 | async-start | bytes 2097152 | tf_op jit(solution)/shard_map/all_to_all | solution.py:410
  98.9 11.3 %copy-start.6 = (s32[4]{0:T(128)S(1)}, s32[4]{0:T(128)}, u32[]{:S(2)}) copy-start(s32[4]{0:T(128)} %pad_add_fusion.ctl_ref) | copy-start | bytes 52
  112.7 1.3 copy-start.2
  115.9 1.5 %copy-start.3 = (bf16[960,1024]{1,0:T(8,128)(2,1)S(1)}, bf16[960,1024]{1,0:T(8,128)(2,1)}, u32[]{:S(2)}) copy-start(bf16[960,1024]{1,0:T(8,128)(2,1)} %copy-done.2) | copy-start | bytes 5898244

commit v4 on v3

--- a/solution.py
+++ b/solution.py
@@ -34,52 +34,64 @@
     )
 
 
-def project_kernel(f_ref, wk_ref, wv_ref, gain_ref, send_ref, pre_ref, total):
-    step, steps = pl.program_id(0), pl.num_programs(0)
+def project_kernel(
+    f_hbm, wk_hbm, wv_hbm, gain_ref, send_ref, pre_ref, f_ref, wk_ref, wv_ref, arrived, *, parts
+):
+    tokens, feat = f_ref.shape
     kv_dim = wk_ref.shape[1]
-
-    @pl.when(step == 0)
-    def _():
-        total[...] = jnp.zeros_like(total)
-
-    total[:, :kv_dim] += jnp.dot(f_ref[...], wk_ref[...], preferred_element_type=F32)
-    total[:, kv_dim:] += jnp.dot(f_ref[...], wv_ref[...], preferred_element_type=F32)
-
-    @pl.when(step == steps - 1)
-    def _():
-        pre_ref[...] = total[:, :kv_dim]
-        for group in range(kv_dim // HEAD_DIM):
-            cols = slice(group * HEAD_DIM, (group + 1) * HEAD_DIM)
-            head = total[:, cols]
-            factor = lax.rsqrt(jnp.mean(head * head, axis=-1, keepdims=True) + EPSILON)
-            key = (head * factor * gain_ref[...]).astype(BF16)
-            start = kv_dim + group * HEAD_DIM
-            value = total[:, start : start + HEAD_DIM].astype(BF16)
-            at = 2 * group * HEAD_DIM
-            for copy in range(send_ref.shape[0]):
-                send_ref[copy, :, at : at + HEAD_DIM] = key
-                send_ref[copy, :, at + HEAD_DIM : at + 2 * HEAD_DIM] = value
+    depth = feat // parts
+    copies = []
+    for part in range(parts):
+        here = pl.ds(part * depth, depth)
+        copies.append(
+            [
+                pltpu.make_async_copy(f_hbm.at[:, here], f_ref.at[:, here], arrived.at[0, part]),
+                pltpu.make_async_copy(wk_hbm.at[here], wk_ref.at[here], arrived.at[1, part]),
+                pltpu.make_async_copy(wv_hbm.at[here], wv_ref.at[here], arrived.at[2, part]),
+            ]
+        )
+    for trio in copies:
+        for copy in trio:
+            copy.start()
+    keys = jnp.zeros((tokens, kv_dim), F32)
+    values = jnp.zeros((tokens, kv_dim), F32)
+    for part, trio in enumerate(copies):
+        here = slice(part * depth, (part + 1) * depth)
+        for copy in trio:
+            copy.wait()
+        left = f_ref[:, here]
+        keys += jnp.dot(left, wk_ref[here], preferred_element_type=F32)
+        values += jnp.dot(left, wv_ref[here], preferred_element_type=F32)
+    pre_ref[...] = keys
+    for group in range(kv_dim // HEAD_DIM):
+        cols = slice(group * HEAD_DIM, (group + 1) * HEAD_DIM)
+        head = keys[:, cols]
+        factor = lax.rsqrt(jnp.mean(head * head, axis=-1, keepdims=True) + EPSILON)
+        key = (head * factor * gain_ref[...]).astype(BF16)
+        value = values[:, cols].astype(BF16)
+        at = 2 * group * HEAD_DIM
+        for copy in range(send_ref.shape[0]):
+            send_ref[copy, :, at : at + HEAD_DIM] = key
+            send_ref[copy, :, at + HEAD_DIM : at + 2 * HEAD_DIM] = value
 
 
 def project(feats, w_key, w_value, gain, copies):
     tokens, feat = feats.shape
     kv_dim = w_key.shape[1]
-    steps = 5
-    depth = feat // steps
+    parts = 6
     send, pre = (copies, tokens, 2 * kv_dim), (tokens, kv_dim)
-    return pl.pallas_call(
-        project_kernel,
-        grid=(steps,),
-        in_specs=[
-            pl.BlockSpec((tokens, depth), lambda k: (0, k)),
-            pl.BlockSpec((depth, kv_dim), lambda k: (k, 0)),
-            pl.BlockSpec((depth, kv_dim), lambda k: (k, 0)),
-            whole((1, HEAD_DIM)),
+    anywhere = pl.BlockSpec(memory_space=pl.ANY)
+    return pl.pallas_call(
+        functools.partial(project_kernel, parts=parts),
+        in_specs=[anywhere, anywhere, anywhere, pl.BlockSpec(memory_space=pltpu.VMEM)],
+        out_shape=[jax.ShapeDtypeStruct(send, BF16), jax.ShapeDtypeStruct(pre, F32)],
+        scratch_shapes=[
+            pltpu.VMEM((tokens, feat), BF16),
+            pltpu.VMEM((feat, kv_dim), BF16),
+            pltpu.VMEM((feat, kv_dim), BF16),
+            pltpu.SemaphoreType.DMA((3, parts)),
         ],
-        out_specs=[whole(send), whole(pre)],
-        out_shape=[jax.ShapeDtypeStruct(send, BF16), jax.ShapeDtypeStruct(pre, F32)],
-        scratch_shapes=[pltpu.VMEM((tokens, 2 * kv_dim), F32)],
-        compiler_params=params(1),
+        compiler_params=params(0),
         cost_estimate=pl.CostEstimate(
             flops=4 * tokens * feat * kv_dim,
             bytes_accessed=4 * feat * kv_dim + 4 * tokens * feat,

time: 138 us -> 136 us (0.986); the launches traced: 137 us -> 136 us
  no operation moved by 1% of the time
where the time goes in v4:
time: 136 us
  Pallas kernels  51 us (38%)
  waiting for transfers between devices  32.1 us (24%)
  starting transfers between devices  28.9 us (21%)
  blocking collectives  17.5 us (13%)
  local copies, waits for them, and re-layouts  4.17 us (3%)
  between operations  2.06 us (2%)
    all_to_all x4, waiting for transfers between devices, exchange(): return lax.all_to_all(array, axes, split_axis=0, concat_axis=0, tiled=True)  32.1 us
    all_to_all x4, starting transfers between devices, exchange(): return lax.all_to_all(array, axes, split_axis=0, concat_axis=0, tiled=True)  28.9 us
    pallas_call x2, Pallas kernels, apply(): pl.pallas_call(functools.partial(apply_kernel, heads=heads, start=start,...  22.4 us
    all_to_all x1, blocking collectives, exchange(): return lax.all_to_all(array, axes, split_axis=0, concat_axis=0, tiled=True)  17.5 us
    pallas_call x1, Pallas kernels, attend(): pl.pallas_call(functools.partial(attend_kernel, heads=heads), grid_spec=p...  15.8 us
    pallas_call x1, Pallas kernels, project(): pl.pallas_call(functools.partial(project_kernel, parts=parts), in_specs=[...  6.06 us
    unnamed x18, local copies, waits for them, and re-layouts  4.17 us
  transfers between devices with their start and end apart: 4, of which 4 were waited for; matrix products, arithmetic and copies ran while one was open for 0% of the time, Pallas kernels for 30%

profile of v4, /device:TPU:0, one launch (start us, length us, event | category | flops | bytes accessed | tf_op | source)
XLA Modules:
  0.0 136.4 jit_solution(11621528076527688812)
XLA Ops:
  0.6 6.1 %project.1 = (bf16[8,128,512]{2,1,0:T(8,128)(2,1)}, f32[128,256]{1,0:T(8,128)}) custom-call(bf16[128,7680]{1,0:T(8,128)(2,1)} %bitcast.16, bf16[7680,256]{1,0:T(8,128)(2,1)} %wk_hbm.1, bf16[7680,256]{1,0:T(8,128)(2,1)} %wv_hbm.1, f32[1,128]{1,0:T(1,128)} %bitcast.20), custom_call_target="tpu_custom_call" | custom-call | flops 1006632960 | bytes 11796480 | tf_op jit(solution)/shard_map/project/pallas_call | solution.py:84
  6.7 0.0 copy-start.1
  6.7 0.0 copy-start.4
  6.7 11.6 %all-to-all-start = ((bf16[64,16,512]{2,1,0:T(8,128)(2,1)}), bf16[64,16,512]{2,1,0:T(8,128)(2,1)S(1)}, u32[]{:S(2)}, u32[]{:S(2)}) async-start(bf16[64,16,512]{2,1,0:T(8,128)(2,1)} %bitcast.27), calls=%async_computation | async-start | bytes 2097152 | tf_op jit(solution)/shard_map/all_to_all | solution.py:422
  18.4 0.0 copy-done.1
  18.4 0.0 copy-done.4
  18.4 0.2 cut.1
  18.6 0.0 copy-start
  18.6 1.3 copy-done
  21.2 0.7 pad_add_fusion.ctl_ref
  21.9 14.5 %all-to-all-done = bf16[64,16,512]{2,1,0:T(8,128)(2,1)S(1)} async-done(((bf16[64,16,512]{2,1,0:T(8,128)(2,1)}), bf16[64,16,512]{2,1,0:T(8,128)(2,1)S(1)}, u32[]{:S(2)}, u32[]{:S(2)}) %all-to-all-start) | async-done | bytes 1048608 | tf_op jit(solution)/shard_map/all_to_all | solution.py:422
  36.4 0.0 copy-start.8
  36.4 3.8 %all-to-all-start.1 = ((bf16[8,128,1024]{2,1,0:T(8,128)(2,1)}), bf16[8,128,1024]{2,1,0:T(8,128)(2,1)S(1)}, u32[]{:S(2)}, u32[]{:S(2)}) async-start(bf16[8,128,1024]{2,1,0:T(8,128)(2,1)} %copy-done), calls=%async_computation.1 | async-start | bytes 4194304 | tf_op jit(solution)/shard_map/all_to_all | solution.py:422
  40.3 0.0 copy-done.8
  40.3 15.8 %attend.1 = (bf16[1024,8192]{1,0:T(8,128)(2,1)}, bf16[1024,8192]{1,0:T(8,128)(2,1)}, bf16[1024,512]{1,0:T(8,128)(2,1)}) custom-call(s32[4]{0:T(128)} %pad_add_fusion.ctl_ref, bf16[512,2048]{1,0:T(8,128)(2,1)} %bitcast.29, bf16[512,2048]{1,0:T(8,128)(2,1)} %bitcast.30, bf16[1024,512]{1,0:T(8,128)(2,1)} %bitcast.22), custom_call_target="tpu_custom_call" | custom-call | flops 21474836480 | bytes 8388608 | tf_op jit(solution)/shard_map/attend/pallas_call | solution.py:228
  56.1 11.3 %all-to-all-done.1 = bf16[8,128,1024]{2,1,0:T(8,128)(2,1)S(1)} async-done(((bf16[8,128,1024]{2,1,0:T(8,128)(2,1)}), bf16[8,128,1024]{2,1,0:T(8,128)(2,1)S(1)}, u32[]{:S(2)}, u32[]{:S(2)}) %all-to-all-start.1) | async-done | bytes 2097184 | tf_op jit(solution)/shard_map/all_to_all | solution.py:422
  67.4 3.7 %all-to-all-start.2 = ((bf16[8,128,512]{2,1,0:T(8,128)(2,1)}), bf16[8,128,512]{2,1,0:T(8,128)(2,1)S(1)}, u32[]{:S(2)}, u32[]{:S(2)}) async-start(bf16[8,128,512]{2,1,0:T(8,128)(2,1)} %bitcast.28), calls=%async_computation.2 | async-start | bytes 2097152 | tf_op jit(solution)/shard_map/all_to_all | solution.py:422
  71.1 0.0 copy-start.5
  71.1 0.0 copy-start.7
  71.2 11.1 %attended.1 = bf16[512,2048]{1,0:T(8,128)(2,1)} custom-call(s32[4]{0:T(128)} %pad_add_fusion.ctl_ref, bf16[1024,8192]{1,0:T(8,128)(2,1)} %get-tuple-element.27.left_ref, bf16[1024,512]{1,0:T(8,128)(2,1)} %bitcast.23), custom_call_target="tpu_custom_call" | custom-call | flops 2147483648 | bytes 16777216 | tf_op jit(solution)/shard_map/attended/pallas_call | solution.py:277
  82.3 4.4 %all-to-all-done.2.parts_ref = bf16[8,128,512]{2,1,0:T(8,128)(2,1)S(1)} async-done(((bf16[8,128,512]{2,1,0:T(8,128)(2,1)}), bf16[8,128,512]{2,1,0:T(8,128)(2,1)S(1)}, u32[]{:S(2)}, u32[]{:S(2)}) %all-to-all-start.2) | async-done | bytes 1048608 | tf_op jit(solution)/shard_map/all_to_all | solution.py:422
  86.7 0.0 copy-done.5
  86.7 0.0 copy-done.7
  86.7 2.0 %norm_back.1 = bf16[8,128,512]{2,1,0:T(8,128)(2,1)} custom-call(s32[4]{0:T(128)S(1)} %copy-done.5, bf16[8,128,512]{2,1,0:T(8,128)(2,1)S(1)} %all-to-all-done.2.parts_ref, bf16[8,8,16,1024]{3,2,1,0:T(8,128)(2,1)S(1)} %bitcast.14, f32[1,128]{1,0:T(1,128)S(1)} %bitcast.21), custom_call_target="tpu_custom_call" | custom-call | tf_op jit(solution)/shard_map/norm_back/pallas_call | solution.py:332
  88.7 9.6 %all-to-all-start.3 = ((bf16[8,128,512]{2,1,0:T(8,128)(2,1)}), bf16[8,128,512]{2,1,0:T(8,128)(2,1)S(1)}, u32[]{:S(2)}, u32[]{:S(2)}) async-start(bf16[8,128,512]{2,1,0:T(8,128)(2,1)} %norm_back.1), calls=%async_computation.3 | async-start | bytes 2097152 | tf_op jit(solution)/shard_map/all_to_all | solution.py:422
  98.3 0.0 copy-start.6
  98.3 11.3 %query_grad.1 = bf16[512,2048]{1,0:T(8,128)(2,1)} custom-call(s32[4]{0:T(128)} %pad_add_fusion.ctl_ref, bf16[1024,8192]{1,0:T(8,128)(2,1)} %get-tuple-element.31.left_ref, bf16[1024,512]{1,0:T(8,128)(2,1)} %bitcast.24), custom_call_target="tpu_custom_call" | custom-call | flops 2147483648 | bytes 16777216 | tf_op jit(solution)/shard_map/query_grad/pallas_call | solution.py:277
  109.6 0.0 copy-done.6
  109.6 2.5 %turn.1.f_ref = bf16[960,1024]{1,0:T(8,128)(2,1)S(1)} custom-call(s32[4]{0:T(128)S(1)} %copy-done.6, bf16[8,8,16,1024]{3,2,1,0:T(8,128)(2,1)S(1)} %bitcast.15), custom_call_target="tpu_custom_call" | custom-call | tf_op jit(solution)/shard_map/turn/pallas_call | solution.py:370
  112.1 0.0 copy-start.2
  112.1 1.3 copy-done.2
  113.4 1.9 %all-to-all-done.3 = bf16[8,128,512]{2,1,0:T(8,128)(2,1)S(1)} async-done(((bf16[8,128,512]{2,1,0:T(8,128)(2,1)}), bf16[8,128,512]{2,1,0:T(8,128)(2,1)S(1)}, u32[]{:S(2)}, u32[]{:S(2)}) %all-to-all-start.3) | async-done | bytes 1048608 | tf_op jit(solution)/shard_map/all_to_all | solution.py:422
  115.4 0.0 copy-start.3
  115.4 1.5 %copy-done.3 = bf16[960,1024]{1,0:T(8,128)(2,1)S(1)} copy-done((bf16[960,1024]{1,0:T(8,128)(2,1)S(1)}, bf16[960,1024]{1,0:T(8,128)(2,1)}, u32[]{:S(2)}) %copy-start.3) | copy-done | bytes 1966104
  116.9 1.2 weight_grad.1
  118.1 17.5 %all_to_all.25.parts_ref = bf16[8,120,512]{2,1,0:T(8,128)(2,1)S(1)} all-to-all(bf16[8,120,512]{2,1,0:T(8,128)(2,1)S(1)} %bitcast.19), channel_id=1, replica_groups=mesh['dp'=8,'seq'=8,'mp'=2] {'seq'}, dimensions={0} | all-to-all | bytes 1966080 | tf_op jit(solution)/shard_map/all_to_all | solution.py:422
  135.6 0.8 finish.1
Async XLA Ops:
  6.7 11.7 %copy-start.1 = (bf16[8,16,7680]{2,1,0:T(8,128)(2,1)S(1)}, bf16[8,16,7680]{2,1,0:T(8,128)(2,1)}, u32[]{:S(2)}) copy-start(bf16[8,16,7680]{2,1,0:T(8,128)(2,1)} %param.9) | copy-start | bytes 5898244
  6.7 11.7 %copy-start.4 = (f32[128,256]{1,0:T(8,128)S(1)}, f32[128,256]{1,0:T(8,128)}, u32[]{:S(2)}) copy-start(f32[128,256]{1,0:T(8,128)} %get-tuple-element.20.pre_ref) | copy-start | bytes 393220
  6.7 29.7 %all-to-all-start = ((bf16[64,16,512]{2,1,0:T(8,128)(2,1)}), bf16[64,16,512]{2,1,0:T(8,128)(2,1)S(1)}, u32[]{:S(2)}, u32[]{:S(2)}) async-start(bf16[64,16,512]{2,1,0:T(8,128)(2,1)} %bitcast.27), calls=%async_computation | async-start | bytes 2097152 | tf_op jit(solution)/shard_map/all_to_all | solution.py:422
  18.6 1.3 copy-start
  36.4 3.9 %copy-start.8 = (bf16[64,16,512]{2,1,0:T(8,128)(2,1)}, bf16[64,16,512]{2,1,0:T(8,128)(2,1)S(1)}, u32[]{:S(2)}) copy-start(bf16[64,16,512]{2,1,0:T(8,128)(2,1)S(1)} %all-to-all-done) | copy-start | bytes 3145732
  36.4 30.9 %all-to-all-start.1 = ((bf16[8,128,1024]{2,1,0:T(8,128)(2,1)}), bf16[8,128,1024]{2,1,0:T(8,128)(2,1)S(1)}, u32[]{:S(2)}, u32[]{:S(2)}) async-start(bf16[8,128,1024]{2,1,0:T(8,128)(2,1)} %copy-done), calls=%async_computation.1 | async-start | bytes 4194304 | tf_op jit(solution)/shard_map/all_to_all | solution.py:422
  67.4 19.3 %all-to-all-start.2 = ((bf16[8,128,512]{2,1,0:T(8,128)(2,1)}), bf16[8,128,512]{2,1,0:T(8,128)(2,1)S(1)}, u32[]{:S(2)}, u32[]{:S(2)}) async-start(bf16[8,128,512]{2,1,0:T(8,128)(2,1)} %bitcast.28), calls=%async_computation.2 | async-start | bytes 2097152 | tf_op jit(solution)/shard_map/all_to_all | solution.py:422
  71.1 15.6 %copy-start.5 = (s32[4]{0:T(128)S(1)}, s32[4]{0:T(128)}, u32[]{:S(2)}) copy-start(s32[4]{0:T(128)} %pad_add_fusion.ctl_ref) | copy-start | bytes 52
  71.1 15.6 %copy-start.7 = (f32[128]{0:T(128)S(1)}, f32[128]{0:T(128)}, u32[]{:S(2)}) copy-start(f32[128]{0:T(128)} %param.12) | copy-start | bytes 1540
  88.7 26.7 %all-to-all-start.3 = ((bf16[8,128,512]{2,1,0:T(8,128)(2,1)}), bf16[8,128,512]{2,1,0:T(8,128)(2,1)S(1)}, u32[]{:S(2)}, u32[]{:S(2)}) async-start(bf16[8,128,512]{2,1,0:T(8,128)(2,1)} %norm_back.1), calls=%async_computation.3 | async-start | bytes 2097152 | tf_op jit(solution)/shard_map/all_to_all | solution.py:422
  98.3 11.3 %copy-start.6 = (s32[4]{0:T(128)S(1)}, s32[4]{0:T(128)}, u32[]{:S(2)}) copy-start(s32[4]{0:T(128)} %pad_add_fusion.ctl_ref) | copy-start | bytes 52
  112.1 1.3 copy-start.2
  115.4 1.5 %copy-start.3 = (bf16[960,1024]{1,0:T(8,128)(2,1)S(1)}, bf16[960,1024]{1,0:T(8,128)(2,1)}, u32[]{:S(2)}) copy-start(bf16[960,1024]{1,0:T(8,128)(2,1)} %copy-done.2) | copy-start | bytes 5898244

commit v5 on v4

--- a/solution.py
+++ b/solution.py
@@ -320,12 +320,11 @@
         inner = jnp.mean(head * gained, axis=-1, keepdims=True)
         pre_grad = (factor * gained - factor * factor * factor * head * inner).astype(BF16)
         value_grad = grad[:, at + HEAD_DIM : at + 2 * HEAD_DIM].astype(BF16)
-        for copy in range(out_ref.shape[0]):
-            out_ref[copy, :, at : at + HEAD_DIM] = pre_grad
-            out_ref[copy, :, at + HEAD_DIM : at + 2 * HEAD_DIM] = value_grad
-
-
-def norm_back(ctl, parts, windows, gain, copies):
+        out_ref[:, at : at + HEAD_DIM] = pre_grad
+        out_ref[:, at + HEAD_DIM : at + 2 * HEAD_DIM] = value_grad
+
+
+def norm_back(ctl, parts, windows, gain):
     tokens, width = parts.shape[1:]
     sources, rows, own, lanes = windows.shape
     last = lanes // LANES - 1
@@ -341,9 +340,9 @@
                 ),
                 whole(gain.shape),
             ],
-            out_specs=whole((copies, tokens, width)),
-        ),
-        out_shape=jax.ShapeDtypeStruct((copies, tokens, width), BF16),
+            out_specs=whole((tokens, width)),
+        ),
+        out_shape=jax.ShapeDtypeStruct((tokens, width), BF16),
         compiler_params=params(1, SMALL_LIMIT),
         name="norm_back",
     )(ctl, parts, windows, gain)
@@ -381,22 +380,34 @@
     )(ctl, windows)
 
 
-def weight_kernel(f_ref, g_ref, out_ref):
-    out_ref[...] = jnp.dot(f_ref[...], g_ref[...], preferred_element_type=F32).astype(BF16)
-
-
-def weight_grad(turned, grads):
+def weight_kernel(ctl_ref, f_ref, *refs):
+    pieces, (out_ref, grads_ref) = refs[:-2], refs[-2:]
+    tokens = pieces[0].shape[0]
+    for away, piece in enumerate(pieces):
+        source = lax.rem(ctl_ref[4] + len(pieces) - away, len(pieces))
+        grads_ref[pl.ds(pl.multiple_of(source * tokens, tokens), tokens)] = piece[...]
+    out_ref[...] = jnp.dot(f_ref[...], grads_ref[...], preferred_element_type=F32).astype(BF16)
+
+
+def weight_grad(ctl, turned, pieces):
     feat, tokens = turned.shape
-    width = grads.shape[1]
+    width = pieces[0].shape[1]
     return pl.pallas_call(
         weight_kernel,
+        grid_spec=pltpu.PrefetchScalarGridSpec(
+            num_scalar_prefetch=1,
+            grid=(1,),
+            in_specs=[whole(turned.shape)] + [whole(piece.shape) for piece in pieces],
+            out_specs=whole((feat, width)),
+            scratch_shapes=[pltpu.VMEM((tokens, width), BF16)],
+        ),
         out_shape=jax.ShapeDtypeStruct((feat, width), BF16),
-        compiler_params=params(0, SMALL_LIMIT),
+        compiler_params=params(1, SMALL_LIMIT),
         cost_estimate=pl.CostEstimate(
             flops=2 * feat * tokens * width, bytes_accessed=2 * feat * tokens, transcendentals=0
         ),
         name="weight_grad",
-    )(turned, grads)
+    )(ctl, turned, *pieces)
 
 
 def finish_kernel(parts_ref, key_ref, value_ref):
@@ -430,7 +441,9 @@
     tokens = rows * own
     gain = key_gain.reshape(1, HEAD_DIM)
     dp_index, seq_index = lax.axis_index("dp"), lax.axis_index("seq")
-    ctl = jnp.stack([tile_counts[0], seq_index * text_dev, text_start[0], dp_index & 1])
+    ctl = jnp.stack(
+        [tile_counts[0], seq_index * text_dev, text_start[0], dp_index & 1, dp_index]
+    )
     feats = features.reshape(tokens, feat)
     send, key_pre = project(feats, w_key, w_value, gain, seq)
     windows = cut(feats, key_pre, dp)
@@ -443,13 +456,16 @@
     shares = exchange(grads.reshape(seq, tokens, pairs), "seq")
     attended = apply(ctl, probs, keys_values, text_dev, HEAD_DIM, True, "attended")
     shares, attended = lax.optimization_barrier((shares, attended))
-    rounded = norm_back(ctl, shares, windows, gain, dp)
-    everywhere = exchange(rounded, "dp").reshape(dp * tokens, pairs)
+    rounded = norm_back(ctl, shares, windows, gain)
+    everywhere = [rounded]
+    for away in range(1, dp):
+        to = [(source, (source + away) % dp) for source in range(dp)]
+        everywhere.append(lax.ppermute(rounded, "dp", to))
     turned = turn(ctl, windows, feat // dp)
+    partial = weight_grad(ctl, turned, everywhere)
+    pieces = exchange(partial.reshape(seq, feat // dp // seq, pairs), "seq")
     query_grad = apply(ctl, score_grads, keys_values, text_dev, 0, False, "query_grad")
-    everywhere, query_grad = lax.optimization_barrier((everywhere, query_grad))
-    partial = weight_grad(turned, everywhere)
-    pieces = exchange(partial.reshape(seq, feat // dp // seq, pairs), "seq")
+    pieces, query_grad = lax.optimization_barrier((pieces, query_grad))
     key_weight, value_weight = finish(pieces)
     return attended[None], query_grad[None], key_weight, value_weight
 

time: 136 us -> 131 us (0.963)
  blocking collectives: 17.5 us -> 0 us
  starting transfers between devices: 28.9 us -> 40.3 us
    all_to_all x1 -> x0, blocking collectives: 17.5 us -> none  [exchange(): return lax.all_to_all(array, axes, split_axis=0, concat_axis=0, tiled=True)]
    ppermute x0 -> x7, starting transfers between devices: none -> 17.5 us  [on_device(): everywhere.append(lax.ppermute(rounded, 'dp', to))]
    all_to_all x4, starting transfers between devices: 28.9 us -> 22.8 us  [exchange(): return lax.all_to_all(array, axes, split_axis=0, concat_axis=0, tiled=True)]
    ppermute x0 -> x7, waiting for transfers between devices: none -> 2.71 us  [on_device(): everywhere.append(lax.ppermute(rounded, 'dp', to))]
    all_to_all x4, waiting for transfers between devices: 32.1 us -> 30.1 us  [exchange(): return lax.all_to_all(array, axes, split_axis=0, concat_axis=0, tiled=True)]
    pallas_call x1, Pallas kernels: 1.17 us -> 2.76 us  [weight_grad(): pl.pallas_call(weight_kernel, grid_spec=pltpu.PrefetchScalarGridSpec(num_...]
    unnamed x18 -> x12, local copies, waits for them, and re-layouts: 4.17 us -> 2.87 us
  transfers between devices with their start and end apart: 4 -> 11, of which waited for: 4 -> 6; matrix products, arithmetic and copies ran while one was open for 0% -> 0% of each run, Pallas kernels for 30% -> 31%
where the time goes in v5:
time: 131 us; the launch traced here: 130 us
  Pallas kernels  51.5 us (39%)
  starting transfers between devices  40.3 us (31%)
  waiting for transfers between devices  32.8 us (25%)
  local copies, waits for them, and re-layouts  3.47 us (3%)
  between operations  2.08 us (2%)
    all_to_all x4, waiting for transfers between devices, exchange(): return lax.all_to_all(array, axes, split_axis=0, concat_axis=0, tiled=True)  30.1 us
    all_to_all x4, starting transfers between devices, exchange(): return lax.all_to_all(array, axes, split_axis=0, concat_axis=0, tiled=True)  22.8 us
    pallas_call x2, Pallas kernels, apply(): pl.pallas_call(functools.partial(apply_kernel, heads=heads, start=start,...  22.4 us
    ppermute x7, starting transfers between devices, on_device(): everywhere.append(lax.ppermute(rounded, 'dp', to))  17.5 us
    pallas_call x1, Pallas kernels, attend(): pl.pallas_call(functools.partial(attend_kernel, heads=heads), grid_spec=p...  16 us
    pallas_call x1, Pallas kernels, project(): pl.pallas_call(functools.partial(project_kernel, parts=parts), in_specs=[...  6.06 us
    unnamed x12, local copies, waits for them, and re-layouts  2.87 us
    pallas_call x1, Pallas kernels, weight_grad(): pl.pallas_call(weight_kernel, grid_spec=pltpu.PrefetchScalarGridSpec(num_...  2.76 us
  transfers between devices with their start and end apart: 11, of which 6 were waited for; matrix products, arithmetic and copies ran while one was open for 0% of the time, Pallas kernels for 31%

profile of v5, /device:TPU:0, one launch (start us, length us, event | category | flops | bytes accessed | tf_op | source)
XLA Modules:
  0.0 130.2 jit_solution(5085390995729063683)
XLA Ops:
  0.6 6.1 %project.1 = (bf16[8,128,512]{2,1,0:T(8,128)(2,1)}, f32[128,256]{1,0:T(8,128)}) custom-call(bf16[128,7680]{1,0:T(8,128)(2,1)} %bitcast.16, bf16[7680,256]{1,0:T(8,128)(2,1)} %wk_hbm.1, bf16[7680,256]{1,0:T(8,128)(2,1)} %wv_hbm.1, f32[1,128]{1,0:T(1,128)} %bitcast.18), custom_call_target="tpu_custom_call" | custom-call | flops 1006632960 | bytes 11796480 | tf_op jit(solution)/shard_map/project/pallas_call | solution.py:84
  6.7 0.0 copy-start.2
  6.7 11.6 %all-to-all-start = ((bf16[64,16,512]{2,1,0:T(8,128)(2,1)}), bf16[64,16,512]{2,1,0:T(8,128)(2,1)S(1)}, u32[]{:S(2)}, u32[]{:S(2)}) async-start(bf16[64,16,512]{2,1,0:T(8,128)(2,1)} %bitcast.25), calls=%async_computation | async-start | bytes 2097152 | tf_op jit(solution)/shard_map/all_to_all | solution.py:433
  19.7 0.0 copy-done.2
  19.7 0.0 copy-start.1
  19.7 1.5 %copy-done.1 = bf16[8,16,7680]{2,1,0:T(8,128)(2,1)S(1)} copy-done((bf16[8,16,7680]{2,1,0:T(8,128)(2,1)S(1)}, bf16[8,16,7680]{2,1,0:T(8,128)(2,1)}, u32[]{:S(2)}) %copy-start.1) | copy-done | bytes 1966104
  21.2 0.2 cut.1
  21.4 0.0 copy-start
  21.4 1.3 %copy-done = bf16[8,128,1024]{2,1,0:T(8,128)(2,1)} copy-done((bf16[8,128,1024]{2,1,0:T(8,128)(2,1)}, bf16[8,128,1024]{2,1,0:T(8,128)(2,1)S(1)}, u32[]{:S(2)}) %copy-start) | copy-done | bytes 2097176
  22.8 0.6 stack.15.ctl_ref
  23.3 13.1 %all-to-all-done = bf16[64,16,512]{2,1,0:T(8,128)(2,1)S(1)} async-done(((bf16[64,16,512]{2,1,0:T(8,128)(2,1)}), bf16[64,16,512]{2,1,0:T(8,128)(2,1)S(1)}, u32[]{:S(2)}, u32[]{:S(2)}) %all-to-all-start) | async-done | bytes 1048608 | tf_op jit(solution)/shard_map/all_to_all | solution.py:433
  36.4 0.0 copy-start.5
  36.4 3.8 %all-to-all-start.1 = ((bf16[8,128,1024]{2,1,0:T(8,128)(2,1)}), bf16[8,128,1024]{2,1,0:T(8,128)(2,1)S(1)}, u32[]{:S(2)}, u32[]{:S(2)}) async-start(bf16[8,128,1024]{2,1,0:T(8,128)(2,1)} %copy-done), calls=%async_computation.1 | async-start | bytes 4194304 | tf_op jit(solution)/shard_map/all_to_all | solution.py:433
  40.3 0.0 copy-done.5
  40.3 16.0 %attend.1 = (bf16[1024,8192]{1,0:T(8,128)(2,1)}, bf16[1024,8192]{1,0:T(8,128)(2,1)}, bf16[1024,512]{1,0:T(8,128)(2,1)}) custom-call(s32[5]{0:T(128)} %stack.15.ctl_ref, bf16[512,2048]{1,0:T(8,128)(2,1)} %bitcast.27, bf16[512,2048]{1,0:T(8,128)(2,1)} %bitcast.28, bf16[1024,512]{1,0:T(8,128)(2,1)} %bitcast.20), custom_call_target="tpu_custom_call" | custom-call | flops 21474836480 | bytes 8388608 | tf_op jit(solution)/shard_map/attend/pallas_call | solution.py:228
  56.2 11.1 %all-to-all-done.1 = bf16[8,128,1024]{2,1,0:T(8,128)(2,1)S(1)} async-done(((bf16[8,128,1024]{2,1,0:T(8,128)(2,1)}), bf16[8,128,1024]{2,1,0:T(8,128)(2,1)S(1)}, u32[]{:S(2)}, u32[]{:S(2)}) %all-to-all-start.1) | async-done | bytes 2097184 | tf_op jit(solution)/shard_map/all_to_all | solution.py:433
  67.4 3.7 %all-to-all-start.2 = ((bf16[8,128,512]{2,1,0:T(8,128)(2,1)}), bf16[8,128,512]{2,1,0:T(8,128)(2,1)S(1)}, u32[]{:S(2)}, u32[]{:S(2)}) async-start(bf16[8,128,512]{2,1,0:T(8,128)(2,1)} %bitcast.26), calls=%async_computation.2 | async-start | bytes 2097152 | tf_op jit(solution)/shard_map/all_to_all | solution.py:433
  71.1 0.0 copy-start.3
  71.1 0.0 copy-start.4
  71.1 11.1 %attended.1 = bf16[512,2048]{1,0:T(8,128)(2,1)} custom-call(s32[5]{0:T(128)} %stack.15.ctl_ref, bf16[1024,8192]{1,0:T(8,128)(2,1)} %get-tuple-element.27.left_ref, bf16[1024,512]{1,0:T(8,128)(2,1)} %bitcast.21), custom_call_target="tpu_custom_call" | custom-call | flops 2147483648 | bytes 16777216 | tf_op jit(solution)/shard_map/attended/pallas_call | solution.py:277
  82.3 4.4 %all-to-all-done.2.parts_ref = bf16[8,128,512]{2,1,0:T(8,128)(2,1)S(1)} async-done(((bf16[8,128,512]{2,1,0:T(8,128)(2,1)}), bf16[8,128,512]{2,1,0:T(8,128)(2,1)S(1)}, u32[]{:S(2)}, u32[]{:S(2)}) %all-to-all-start.2) | async-done | bytes 1048608 | tf_op jit(solution)/shard_map/all_to_all | solution.py:433
  86.7 0.0 copy-done.3
  86.7 0.0 copy-done.4
  86.7 0.9 norm_back.1.refs_0_
  87.6 0.1 collective-permute-start
  87.7 2.4 %collective-permute-start.1 = (bf16[128,512]{1,0:T(8,128)(2,1)S(1)}, bf16[128,512]{1,0:T(8,128)(2,1)S(1)}, u32[]{:S(2)}, u32[]{:S(2)}) collective-permute-start(bf16[128,512]{1,0:T(8,128)(2,1)S(1)} %norm_back.1.refs_0_), channel_id=1, source_target_pairs={{0,32},{16,48},{32,64},{48,80},{64,96},{80,112},{96,0},{112,16},{1... | collective-permute-start | bytes 393224 | tf_op jit(solution)/shard_map/ppermute | solution.py:463
  90.1 8.7 %collective-permute-start.2 = (bf16[128,512]{1,0:T(8,128)(2,1)S(1)}, bf16[128,512]{1,0:T(8,128)(2,1)S(1)}, u32[]{:S(2)}, u32[]{:S(2)}) collective-permute-start(bf16[128,512]{1,0:T(8,128)(2,1)S(1)} %norm_back.1.refs_0_), channel_id=1, source_target_pairs={{0,48},{16,64},{32,80},{48,96},{64,112},{80,0},{96,16},{112,32},{1... | collective-permute-start | bytes 393224 | tf_op jit(solution)/shard_map/ppermute | solution.py:463
  98.7 0.0 collective-permute-start.3
  98.8 2.4 %collective-permute-start.4 = (bf16[128,512]{1,0:T(8,128)(2,1)S(1)}, bf16[128,512]{1,0:T(8,128)(2,1)S(1)}, u32[]{:S(2)}, u32[]{:S(2)}) collective-permute-start(bf16[128,512]{1,0:T(8,128)(2,1)S(1)} %norm_back.1.refs_0_), channel_id=1, source_target_pairs={{0,80},{16,96},{32,112},{48,0},{64,16},{80,32},{96,48},{112,64},{1... | collective-permute-start | bytes 393224 | tf_op jit(solution)/shard_map/ppermute | solution.py:463
  101.2 0.0 collective-permute-done.refs_1_
  101.2 3.8 %collective-permute-start.5 = (bf16[128,512]{1,0:T(8,128)(2,1)S(1)}, bf16[128,512]{1,0:T(8,128)(2,1)S(1)}, u32[]{:S(2)}, u32[]{:S(2)}) collective-permute-start(bf16[128,512]{1,0:T(8,128)(2,1)S(1)} %norm_back.1.refs_0_), channel_id=1, source_target_pairs={{0,96},{16,112},{32,0},{48,16},{64,32},{80,48},{96,64},{112,80},{1... | collective-permute-start | bytes 393224 | tf_op jit(solution)/shard_map/ppermute | solution.py:463
  105.0 0.0 collective-permute-done.1.refs_2_
  105.0 0.2 collective-permute-start.6
  105.1 2.5 %turn.1.f_ref = bf16[960,1024]{1,0:T(8,128)(2,1)S(1)} custom-call(s32[5]{0:T(128)S(1)} %copy-done.3, bf16[8,8,16,1024]{3,2,1,0:T(8,128)(2,1)S(1)} %bitcast.15), custom_call_target="tpu_custom_call" | custom-call | tf_op jit(solution)/shard_map/turn/pallas_call | solution.py:369
  107.6 0.0 collective-permute-done.2.refs_3_
  107.6 0.0 collective-permute-done.3.refs_4_
  107.6 0.0 collective-permute-done.4.refs_5_
  107.6 0.5 collective-permute-done.5.refs_6_
  108.2 2.2 %collective-permute-done.6.refs_7_ = bf16[128,512]{1,0:T(8,128)(2,1)S(1)} collective-permute-done((bf16[128,512]{1,0:T(8,128)(2,1)S(1)}, bf16[128,512]{1,0:T(8,128)(2,1)S(1)}, u32[]{:S(2)}, u32[]{:S(2)}) %collective-permute-start.6) | collective-permute-done | bytes 131104 | tf_op jit(solution)/shard_map/ppermute | solution.py:463
  110.3 2.8 %weight_grad.1 = bf16[960,512]{1,0:T(8,128)(2,1)} custom-call(s32[5]{0:T(128)S(1)} %copy-done.3, bf16[960,1024]{1,0:T(8,128)(2,1)S(1)} %turn.1.f_ref, bf16[128,512]{1,0:T(8,128)(2,1)S(1)} %norm_back.1.refs_0_, bf16[128,512]{1,0:T(8,128)(2,1)S(1)} %collective-permute-done.refs_1_, bf16[128,512]{1,0:T(8,128)(2,1)S(1)} %collective-permute-done.1.refs_2_, ...), custom_call_target="tpu_custom_call" | custom-call | flops 1006632960 | bytes 1966080 | tf_op jit(solution)/shard_map/weight_grad/pallas_call | solution.py:395
  113.1 3.6 %all-to-all-start.3 = ((bf16[8,120,512]{2,1,0:T(8,128)(2,1)}), bf16[8,120,512]{2,1,0:T(8,128)(2,1)S(1)}, u32[]{:S(2)}, u32[]{:S(2)}) async-start(bf16[8,120,512]{2,1,0:T(8,128)(2,1)} %bitcast.12), calls=%async_computation.3 | async-start | bytes 1966080 | tf_op jit(solution)/shard_map/all_to_all | solution.py:433
  116.7 11.2 %query_grad.1 = bf16[512,2048]{1,0:T(8,128)(2,1)} custom-call(s32[5]{0:T(128)} %stack.15.ctl_ref, bf16[1024,8192]{1,0:T(8,128)(2,1)} %get-tuple-element.31.left_ref, bf16[1024,512]{1,0:T(8,128)(2,1)} %bitcast.22), custom_call_target="tpu_custom_call" | custom-call | flops 2147483648 | bytes 16777216 | tf_op jit(solution)/shard_map/query_grad/pallas_call | solution.py:277
  127.9 1.5 %all-to-all-done.3.parts_ref = bf16[8,120,512]{2,1,0:T(8,128)(2,1)S(1)} async-done(((bf16[8,120,512]{2,1,0:T(8,128)(2,1)}), bf16[8,120,512]{2,1,0:T(8,128)(2,1)S(1)}, u32[]{:S(2)}, u32[]{:S(2)}) %all-to-all-start.3) | async-done | bytes 983072 | tf_op jit(solution)/shard_map/all_to_all | solution.py:433
  129.4 0.8 finish.1
Async XLA Ops:
  6.7 13.0 %copy-start.2 = (f32[128,256]{1,0:T(8,128)S(1)}, f32[128,256]{1,0:T(8,128)}, u32[]{:S(2)}) copy-start(f32[128,256]{1,0:T(8,128)} %get-tuple-element.20.pre_ref) | copy-start | bytes 393220
  6.7 29.7 %all-to-all-start = ((bf16[64,16,512]{2,1,0:T(8,128)(2,1)}), bf16[64,16,512]{2,1,0:T(8,128)(2,1)S(1)}, u32[]{:S(2)}, u32[]{:S(2)}) async-start(bf16[64,16,512]{2,1,0:T(8,128)(2,1)} %bitcast.25), calls=%async_computation | async-start | bytes 2097152 | tf_op jit(solution)/shard_map/all_to_all | solution.py:433
  19.7 1.5 %copy-start.1 = (bf16[8,16,7680]{2,1,0:T(8,128)(2,1)S(1)}, bf16[8,16,7680]{2,1,0:T(8,128)(2,1)}, u32[]{:S(2)}) copy-start(bf16[8,16,7680]{2,1,0:T(8,128)(2,1)} %param.9) | copy-start | bytes 5898244
  21.4 1.3 %copy-start = (bf16[8,128,1024]{2,1,0:T(8,128)(2,1)}, bf16[8,128,1024]{2,1,0:T(8,128)(2,1)S(1)}, u32[]{:S(2)}) copy-start(bf16[8,128,1024]{2,1,0:T(8,128)(2,1)S(1)} %cut.1) | copy-start | bytes 6291460
  36.4 3.9 %copy-start.5 = (bf16[64,16,512]{2,1,0:T(8,128)(2,1)}, bf16[64,16,512]{2,1,0:T(8,128)(2,1)S(1)}, u32[]{:S(2)}) copy-start(bf16[64,16,512]{2,1,0:T(8,128)(2,1)S(1)} %all-to-all-done) | copy-start | bytes 3145732
  36.4 30.9 %all-to-all-start.1 = ((bf16[8,128,1024]{2,1,0:T(8,128)(2,1)}), bf16[8,128,1024]{2,1,0:T(8,128)(2,1)S(1)}, u32[]{:S(2)}, u32[]{:S(2)}) async-start(bf16[8,128,1024]{2,1,0:T(8,128)(2,1)} %copy-done), calls=%async_computation.1 | async-start | bytes 4194304 | tf_op jit(solution)/shard_map/all_to_all | solution.py:433
  67.4 19.3 %all-to-all-start.2 = ((bf16[8,128,512]{2,1,0:T(8,128)(2,1)}), bf16[8,128,512]{2,1,0:T(8,128)(2,1)S(1)}, u32[]{:S(2)}, u32[]{:S(2)}) async-start(bf16[8,128,512]{2,1,0:T(8,128)(2,1)} %bitcast.26), calls=%async_computation.2 | async-start | bytes 2097152 | tf_op jit(solution)/shard_map/all_to_all | solution.py:433
  71.1 15.6 %copy-start.3 = (s32[5]{0:T(128)S(1)}, s32[5]{0:T(128)}, u32[]{:S(2)}) copy-start(s32[5]{0:T(128)} %stack.15.ctl_ref) | copy-start | bytes 64
  71.1 15.6 %copy-start.4 = (f32[128]{0:T(128)S(1)}, f32[128]{0:T(128)}, u32[]{:S(2)}) copy-start(f32[128]{0:T(128)} %param.12) | copy-start | bytes 1540
  87.6 13.6 %collective-permute-start = (bf16[128,512]{1,0:T(8,128)(2,1)S(1)}, bf16[128,512]{1,0:T(8,128)(2,1)S(1)}, u32[]{:S(2)}, u32[]{:S(2)}) collective-permute-start(bf16[128,512]{1,0:T(8,128)(2,1)S(1)} %norm_back.1.refs_0_), channel_id=1, source_target_pairs={{0,16},{16,32},{32,48},{48,64},{64,80},{80,96},{96,112},{112,0},{1... | collective-permute-start | bytes 393224 | tf_op jit(solution)/shard_map/ppermute | solution.py:463
  87.7 17.3 %collective-permute-start.1 = (bf16[128,512]{1,0:T(8,128)(2,1)S(1)}, bf16[128,512]{1,0:T(8,128)(2,1)S(1)}, u32[]{:S(2)}, u32[]{:S(2)}) collective-permute-start(bf16[128,512]{1,0:T(8,128)(2,1)S(1)} %norm_back.1.refs_0_), channel_id=1, source_target_pairs={{0,32},{16,48},{32,64},{48,80},{64,96},{80,112},{96,0},{112,16},{1... | collective-permute-start | bytes 393224 | tf_op jit(solution)/shard_map/ppermute | solution.py:463
  90.1 17.6 %collective-permute-start.2 = (bf16[128,512]{1,0:T(8,128)(2,1)S(1)}, bf16[128,512]{1,0:T(8,128)(2,1)S(1)}, u32[]{:S(2)}, u32[]{:S(2)}) collective-permute-start(bf16[128,512]{1,0:T(8,128)(2,1)S(1)} %norm_back.1.refs_0_), channel_id=1, source_target_pairs={{0,48},{16,64},{32,80},{48,96},{64,112},{80,0},{96,16},{112,32},{1... | collective-permute-start | bytes 393224 | tf_op jit(solution)/shard_map/ppermute | solution.py:463
  98.7 8.9 %collective-permute-start.3 = (bf16[128,512]{1,0:T(8,128)(2,1)S(1)}, bf16[128,512]{1,0:T(8,128)(2,1)S(1)}, u32[]{:S(2)}, u32[]{:S(2)}) collective-permute-start(bf16[128,512]{1,0:T(8,128)(2,1)S(1)} %norm_back.1.refs_0_), channel_id=1, source_target_pairs={{0,64},{16,80},{32,96},{48,112},{64,0},{80,16},{96,32},{112,48},{1... | collective-permute-start | bytes 393224 | tf_op jit(solution)/shard_map/ppermute | solution.py:463
  98.8 8.9 %collective-permute-start.4 = (bf16[128,512]{1,0:T(8,128)(2,1)S(1)}, bf16[128,512]{1,0:T(8,128)(2,1)S(1)}, u32[]{:S(2)}, u32[]{:S(2)}) collective-permute-start(bf16[128,512]{1,0:T(8,128)(2,1)S(1)} %norm_back.1.refs_0_), channel_id=1, source_target_pairs={{0,80},{16,96},{32,112},{48,0},{64,16},{80,32},{96,48},{112,64},{1... | collective-permute-start | bytes 393224 | tf_op jit(solution)/shard_map/ppermute | solution.py:463
  101.2 7.0 %collective-permute-start.5 = (bf16[128,512]{1,0:T(8,128)(2,1)S(1)}, bf16[128,512]{1,0:T(8,128)(2,1)S(1)}, u32[]{:S(2)}, u32[]{:S(2)}) collective-permute-start(bf16[128,512]{1,0:T(8,128)(2,1)S(1)} %norm_back.1.refs_0_), channel_id=1, source_target_pairs={{0,96},{16,112},{32,0},{48,16},{64,32},{80,48},{96,64},{112,80},{1... | collective-permute-start | bytes 393224 | tf_op jit(solution)/shard_map/ppermute | solution.py:463
  105.0 5.4 %collective-permute-start.6 = (bf16[128,512]{1,0:T(8,128)(2,1)S(1)}, bf16[128,512]{1,0:T(8,128)(2,1)S(1)}, u32[]{:S(2)}, u32[]{:S(2)}) collective-permute-start(bf16[128,512]{1,0:T(8,128)(2,1)S(1)} %norm_back.1.refs_0_), channel_id=1, source_target_pairs={{0,112},{16,0},{32,16},{48,32},{64,48},{80,64},{96,80},{112,96},{1... | collective-permute-start | bytes 393224 | tf_op jit(solution)/shard_map/ppermute | solution.py:463
  113.1 16.3 %all-to-all-start.3 = ((bf16[8,120,512]{2,1,0:T(8,128)(2,1)}), bf16[8,120,512]{2,1,0:T(8,128)(2,1)S(1)}, u32[]{:S(2)}, u32[]{:S(2)}) async-start(bf16[8,120,512]{2,1,0:T(8,128)(2,1)} %bitcast.12), calls=%async_computation.3 | async-start | bytes 1966080 | tf_op jit(solution)/shard_map/all_to_all | solution.py:433

commit v6 on v5

--- a/solution.py
+++ b/solution.py
@@ -271,7 +271,7 @@
 def apply(ctl, left, keys_values, rows, start, masked, name):
     img, pairs = keys_values.shape
     groups = pairs // (2 * HEAD_DIM)
-    heads = 2
+    heads = 4
     all_heads = left.shape[1] // rows
     steps = all_heads // groups // heads
     return pl.pallas_call(

time: 131 us -> 133 us (1.015); the launches traced: 130 us -> 131 us
  Pallas kernels: 51.5 us -> 63.7 us
  waiting for transfers between devices: 32.8 us -> 25.1 us
  starting transfers between devices: 40.3 us -> 36.2 us
    pallas_call x1, Pallas kernels: 16 us -> 31 us  [attend(): pl.pallas_call(functools.partial(attend_kernel, heads=heads), grid_spec=p...]
    all_to_all x4, waiting for transfers between devices: 30.1 us -> 20.7 us  [exchange(): return lax.all_to_all(array, axes, split_axis=0, concat_axis=0, tiled=True)]
    ppermute x7, starting transfers between devices: 17.5 us -> 13.5 us  [on_device(): everywhere.append(lax.ppermute(rounded, 'dp', to))]
    pallas_call x2, Pallas kernels: 22.4 us -> 19.5 us  [apply(): pl.pallas_call(functools.partial(apply_kernel, heads=heads, start=start,...]
    ppermute x7, waiting for transfers between devices: 2.71 us -> 4.39 us  [on_device(): everywhere.append(lax.ppermute(rounded, 'dp', to))]
  transfers between devices with their start and end apart: 11 -> 11, of which waited for: 6 -> 5; matrix products, arithmetic and copies ran while one was open for 0% -> 0% of each run, Pallas kernels for 31% -> 41%
where the time goes in v6:
time: 133 us; the launch traced here: 131 us
  Pallas kernels  63.7 us (48%)
  starting transfers between devices  36.2 us (27%)
  waiting for transfers between devices  25.1 us (19%)
  local copies, waits for them, and re-layouts  3.47 us (3%)
  between operations  2.07 us (2%)
    pallas_call x1, Pallas kernels, attend(): pl.pallas_call(functools.partial(attend_kernel, heads=heads), grid_spec=p...  31 us
    all_to_all x4, starting transfers between devices, exchange(): return lax.all_to_all(array, axes, split_axis=0, concat_axis=0, tiled=True)  22.8 us
    all_to_all x4, waiting for transfers between devices, exchange(): return lax.all_to_all(array, axes, split_axis=0, concat_axis=0, tiled=True)  20.7 us
    pallas_call x2, Pallas kernels, apply(): pl.pallas_call(functools.partial(apply_kernel, heads=heads, start=start,...  19.5 us
    ppermute x7, starting transfers between devices, on_device(): everywhere.append(lax.ppermute(rounded, 'dp', to))  13.5 us
    pallas_call x1, Pallas kernels, project(): pl.pallas_call(functools.partial(project_kernel, parts=parts), in_specs=[...  6.06 us
    ppermute x7, waiting for transfers between devices, on_device(): everywhere.append(lax.ppermute(rounded, 'dp', to))  4.39 us
    unnamed x12, local copies, waits for them, and re-layouts  2.87 us
  transfers between devices with their start and end apart: 11, of which 5 were waited for; matrix products, arithmetic and copies ran while one was open for 0% of the time, Pallas kernels for 41%

profile of v6, /device:TPU:0, one launch (start us, length us, event | category | flops | bytes accessed | tf_op | source)
XLA Modules:
  0.0 130.6 jit_solution(15735319277876071862)
XLA Ops:
  0.6 6.1 %project.1 = (bf16[8,128,512]{2,1,0:T(8,128)(2,1)}, f32[128,256]{1,0:T(8,128)}) custom-call(bf16[128,7680]{1,0:T(8,128)(2,1)} %bitcast.16, bf16[7680,256]{1,0:T(8,128)(2,1)} %wk_hbm.1, bf16[7680,256]{1,0:T(8,128)(2,1)} %wv_hbm.1, f32[1,128]{1,0:T(1,128)} %bitcast.18), custom_call_target="tpu_custom_call" | custom-call | flops 1006632960 | bytes 11796480 | tf_op jit(solution)/shard_map/project/pallas_call | solution.py:84
  6.7 0.0 copy-start.2
  6.7 11.6 %all-to-all-start = ((bf16[64,16,512]{2,1,0:T(8,128)(2,1)}), bf16[64,16,512]{2,1,0:T(8,128)(2,1)S(1)}, u32[]{:S(2)}, u32[]{:S(2)}) async-start(bf16[64,16,512]{2,1,0:T(8,128)(2,1)} %bitcast.25), calls=%async_computation | async-start | bytes 2097152 | tf_op jit(solution)/shard_map/all_to_all | solution.py:433
  19.7 0.0 copy-done.2
  19.7 0.0 copy-start.1
  19.7 1.5 %copy-done.1 = bf16[8,16,7680]{2,1,0:T(8,128)(2,1)S(1)} copy-done((bf16[8,16,7680]{2,1,0:T(8,128)(2,1)S(1)}, bf16[8,16,7680]{2,1,0:T(8,128)(2,1)}, u32[]{:S(2)}) %copy-start.1) | copy-done | bytes 1966104
  21.2 0.2 cut.1
  21.4 0.0 copy-start
  21.4 1.3 %copy-done = bf16[8,128,1024]{2,1,0:T(8,128)(2,1)} copy-done((bf16[8,128,1024]{2,1,0:T(8,128)(2,1)}, bf16[8,128,1024]{2,1,0:T(8,128)(2,1)S(1)}, u32[]{:S(2)}) %copy-start) | copy-done | bytes 2097176
  22.8 0.6 stack.15.ctl_ref
  23.3 13.1 %all-to-all-done = bf16[64,16,512]{2,1,0:T(8,128)(2,1)S(1)} async-done(((bf16[64,16,512]{2,1,0:T(8,128)(2,1)}), bf16[64,16,512]{2,1,0:T(8,128)(2,1)S(1)}, u32[]{:S(2)}, u32[]{:S(2)}) %all-to-all-start) | async-done | bytes 1048608 | tf_op jit(solution)/shard_map/all_to_all | solution.py:433
  36.4 0.0 copy-start.5
  36.4 3.8 %all-to-all-start.1 = ((bf16[8,128,1024]{2,1,0:T(8,128)(2,1)}), bf16[8,128,1024]{2,1,0:T(8,128)(2,1)S(1)}, u32[]{:S(2)}, u32[]{:S(2)}) async-start(bf16[8,128,1024]{2,1,0:T(8,128)(2,1)} %copy-done), calls=%async_computation.1 | async-start | bytes 4194304 | tf_op jit(solution)/shard_map/all_to_all | solution.py:433
  40.3 0.0 copy-done.5
  40.3 31.0 %attend.1 = (bf16[1024,8192]{1,0:T(8,128)(2,1)}, bf16[1024,8192]{1,0:T(8,128)(2,1)}, bf16[1024,512]{1,0:T(8,128)(2,1)}) custom-call(s32[5]{0:T(128)} %stack.15.ctl_ref, bf16[512,2048]{1,0:T(8,128)(2,1)} %bitcast.27, bf16[512,2048]{1,0:T(8,128)(2,1)} %bitcast.28, bf16[1024,512]{1,0:T(8,128)(2,1)} %bitcast.20), custom_call_target="tpu_custom_call" | custom-call | flops 21474836480 | bytes 8388608 | tf_op jit(solution)/shard_map/attend/pallas_call | solution.py:228
  71.3 0.0 all-to-all-done.1
  71.3 3.7 %all-to-all-start.2 = ((bf16[8,128,512]{2,1,0:T(8,128)(2,1)}), bf16[8,128,512]{2,1,0:T(8,128)(2,1)S(1)}, u32[]{:S(2)}, u32[]{:S(2)}) async-start(bf16[8,128,512]{2,1,0:T(8,128)(2,1)} %bitcast.26), calls=%async_computation.2 | async-start | bytes 2097152 | tf_op jit(solution)/shard_map/all_to_all | solution.py:433
  75.1 0.0 copy-start.3
  75.1 0.0 copy-start.4
  75.1 9.8 %attended.1 = bf16[512,2048]{1,0:T(8,128)(2,1)} custom-call(s32[5]{0:T(128)} %stack.15.ctl_ref, bf16[1024,8192]{1,0:T(8,128)(2,1)} %get-tuple-element.27.left_ref, bf16[1024,512]{1,0:T(8,128)(2,1)} %bitcast.21), custom_call_target="tpu_custom_call" | custom-call | flops 2147483648 | bytes 16777216 | tf_op jit(solution)/shard_map/attended/pallas_call | solution.py:277
  84.9 4.3 %all-to-all-done.2.parts_ref = bf16[8,128,512]{2,1,0:T(8,128)(2,1)S(1)} async-done(((bf16[8,128,512]{2,1,0:T(8,128)(2,1)}), bf16[8,128,512]{2,1,0:T(8,128)(2,1)S(1)}, u32[]{:S(2)}, u32[]{:S(2)}) %all-to-all-start.2) | async-done | bytes 1048608 | tf_op jit(solution)/shard_map/all_to_all | solution.py:433
  89.2 0.0 copy-done.3
  89.2 0.0 copy-done.4
  89.2 0.9 norm_back.1.refs_0_
  90.1 1.8 %collective-permute-start = (bf16[128,512]{1,0:T(8,128)(2,1)S(1)}, bf16[128,512]{1,0:T(8,128)(2,1)S(1)}, u32[]{:S(2)}, u32[]{:S(2)}) collective-permute-start(bf16[128,512]{1,0:T(8,128)(2,1)S(1)} %norm_back.1.refs_0_), channel_id=1, source_target_pairs={{0,16},{16,32},{32,48},{48,64},{64,80},{80,96},{96,112},{112,0},{1... | collective-permute-start | bytes 393224 | tf_op jit(solution)/shard_map/ppermute | solution.py:463
  91.9 0.0 collective-permute-start.1
  91.9 4.5 %collective-permute-start.2 = (bf16[128,512]{1,0:T(8,128)(2,1)S(1)}, bf16[128,512]{1,0:T(8,128)(2,1)S(1)}, u32[]{:S(2)}, u32[]{:S(2)}) collective-permute-start(bf16[128,512]{1,0:T(8,128)(2,1)S(1)} %norm_back.1.refs_0_), channel_id=1, source_target_pairs={{0,48},{16,64},{32,80},{48,96},{64,112},{80,0},{96,16},{112,32},{1... | collective-permute-start | bytes 393224 | tf_op jit(solution)/shard_map/ppermute | solution.py:463
  96.4 1.2 collective-permute-start.3
  97.6 2.6 %collective-permute-start.4 = (bf16[128,512]{1,0:T(8,128)(2,1)S(1)}, bf16[128,512]{1,0:T(8,128)(2,1)S(1)}, u32[]{:S(2)}, u32[]{:S(2)}) collective-permute-start(bf16[128,512]{1,0:T(8,128)(2,1)S(1)} %norm_back.1.refs_0_), channel_id=1, source_target_pairs={{0,80},{16,96},{32,112},{48,0},{64,16},{80,32},{96,48},{112,64},{1... | collective-permute-start | bytes 393224 | tf_op jit(solution)/shard_map/ppermute | solution.py:463
  100.2 3.8 %collective-permute-done.refs_1_ = bf16[128,512]{1,0:T(8,128)(2,1)S(1)} collective-permute-done((bf16[128,512]{1,0:T(8,128)(2,1)S(1)}, bf16[128,512]{1,0:T(8,128)(2,1)S(1)}, u32[]{:S(2)}, u32[]{:S(2)}) %collective-permute-start) | collective-permute-done | bytes 131104 | tf_op jit(solution)/shard_map/ppermute | solution.py:463
  104.0 0.2 collective-permute-start.5
  104.2 0.0 collective-permute-done.1.refs_2_
  104.2 3.2 %collective-permute-start.6 = (bf16[128,512]{1,0:T(8,128)(2,1)S(1)}, bf16[128,512]{1,0:T(8,128)(2,1)S(1)}, u32[]{:S(2)}, u32[]{:S(2)}) collective-permute-start(bf16[128,512]{1,0:T(8,128)(2,1)S(1)} %norm_back.1.refs_0_), channel_id=1, source_target_pairs={{0,112},{16,0},{32,16},{48,32},{64,48},{80,64},{96,80},{112,96},{1... | collective-permute-start | bytes 393224 | tf_op jit(solution)/shard_map/ppermute | solution.py:463
  107.3 2.5 %turn.1.f_ref = bf16[960,1024]{1,0:T(8,128)(2,1)S(1)} custom-call(s32[5]{0:T(128)S(1)} %copy-done.3, bf16[8,8,16,1024]{3,2,1,0:T(8,128)(2,1)S(1)} %bitcast.15), custom_call_target="tpu_custom_call" | custom-call | tf_op jit(solution)/shard_map/turn/pallas_call | solution.py:369
  109.8 0.0 collective-permute-done.2.refs_3_
  109.8 0.0 collective-permute-done.3.refs_4_
  109.8 0.0 collective-permute-done.4.refs_5_
  109.8 0.6 collective-permute-done.5.refs_6_
  110.5 0.0 collective-permute-done.6.refs_7_
  110.5 2.8 %weight_grad.1 = bf16[960,512]{1,0:T(8,128)(2,1)} custom-call(s32[5]{0:T(128)S(1)} %copy-done.3, bf16[960,1024]{1,0:T(8,128)(2,1)S(1)} %turn.1.f_ref, bf16[128,512]{1,0:T(8,128)(2,1)S(1)} %norm_back.1.refs_0_, bf16[128,512]{1,0:T(8,128)(2,1)S(1)} %collective-permute-done.refs_1_, bf16[128,512]{1,0:T(8,128)(2,1)S(1)} %collective-permute-done.1.refs_2_, ...), custom_call_target="tpu_custom_call" | custom-call | flops 1006632960 | bytes 1966080 | tf_op jit(solution)/shard_map/weight_grad/pallas_call | solution.py:395
  113.2 3.6 %all-to-all-start.3 = ((bf16[8,120,512]{2,1,0:T(8,128)(2,1)}), bf16[8,120,512]{2,1,0:T(8,128)(2,1)S(1)}, u32[]{:S(2)}, u32[]{:S(2)}) async-start(bf16[8,120,512]{2,1,0:T(8,128)(2,1)} %bitcast.12), calls=%async_computation.3 | async-start | bytes 1966080 | tf_op jit(solution)/shard_map/all_to_all | solution.py:433
  116.8 9.7 %query_grad.1 = bf16[512,2048]{1,0:T(8,128)(2,1)} custom-call(s32[5]{0:T(128)} %stack.15.ctl_ref, bf16[1024,8192]{1,0:T(8,128)(2,1)} %get-tuple-element.31.left_ref, bf16[1024,512]{1,0:T(8,128)(2,1)} %bitcast.22), custom_call_target="tpu_custom_call" | custom-call | flops 2147483648 | bytes 16777216 | tf_op jit(solution)/shard_map/query_grad/pallas_call | solution.py:277
  126.5 3.3 %all-to-all-done.3.parts_ref = bf16[8,120,512]{2,1,0:T(8,128)(2,1)S(1)} async-done(((bf16[8,120,512]{2,1,0:T(8,128)(2,1)}), bf16[8,120,512]{2,1,0:T(8,128)(2,1)S(1)}, u32[]{:S(2)}, u32[]{:S(2)}) %all-to-all-start.3) | async-done | bytes 983072 | tf_op jit(solution)/shard_map/all_to_all | solution.py:433
  129.8 0.8 finish.1
Async XLA Ops:
  6.7 13.0 %copy-start.2 = (f32[128,256]{1,0:T(8,128)S(1)}, f32[128,256]{1,0:T(8,128)}, u32[]{:S(2)}) copy-start(f32[128,256]{1,0:T(8,128)} %get-tuple-element.20.pre_ref) | copy-start | bytes 393220
  6.7 29.7 %all-to-all-start = ((bf16[64,16,512]{2,1,0:T(8,128)(2,1)}), bf16[64,16,512]{2,1,0:T(8,128)(2,1)S(1)}, u32[]{:S(2)}, u32[]{:S(2)}) async-start(bf16[64,16,512]{2,1,0:T(8,128)(2,1)} %bitcast.25), calls=%async_computation | async-start | bytes 2097152 | tf_op jit(solution)/shard_map/all_to_all | solution.py:433
  19.7 1.5 %copy-start.1 = (bf16[8,16,7680]{2,1,0:T(8,128)(2,1)S(1)}, bf16[8,16,7680]{2,1,0:T(8,128)(2,1)}, u32[]{:S(2)}) copy-start(bf16[8,16,7680]{2,1,0:T(8,128)(2,1)} %param.9) | copy-start | bytes 5898244
  21.4 1.3 %copy-start = (bf16[8,128,1024]{2,1,0:T(8,128)(2,1)}, bf16[8,128,1024]{2,1,0:T(8,128)(2,1)S(1)}, u32[]{:S(2)}) copy-start(bf16[8,128,1024]{2,1,0:T(8,128)(2,1)S(1)} %cut.1) | copy-start | bytes 6291460
  36.4 3.9 %copy-start.5 = (bf16[64,16,512]{2,1,0:T(8,128)(2,1)}, bf16[64,16,512]{2,1,0:T(8,128)(2,1)S(1)}, u32[]{:S(2)}) copy-start(bf16[64,16,512]{2,1,0:T(8,128)(2,1)S(1)} %all-to-all-done) | copy-start | bytes 3145732
  36.4 34.9 %all-to-all-start.1 = ((bf16[8,128,1024]{2,1,0:T(8,128)(2,1)}), bf16[8,128,1024]{2,1,0:T(8,128)(2,1)S(1)}, u32[]{:S(2)}, u32[]{:S(2)}) async-start(bf16[8,128,1024]{2,1,0:T(8,128)(2,1)} %copy-done), calls=%async_computation.1 | async-start | bytes 4194304 | tf_op jit(solution)/shard_map/all_to_all | solution.py:433
  71.3 17.9 %all-to-all-start.2 = ((bf16[8,128,512]{2,1,0:T(8,128)(2,1)}), bf16[8,128,512]{2,1,0:T(8,128)(2,1)S(1)}, u32[]{:S(2)}, u32[]{:S(2)}) async-start(bf16[8,128,512]{2,1,0:T(8,128)(2,1)} %bitcast.26), calls=%async_computation.2 | async-start | bytes 2097152 | tf_op jit(solution)/shard_map/all_to_all | solution.py:433
  75.1 14.1 %copy-start.3 = (s32[5]{0:T(128)S(1)}, s32[5]{0:T(128)}, u32[]{:S(2)}) copy-start(s32[5]{0:T(128)} %stack.15.ctl_ref) | copy-start | bytes 64
  75.1 14.1 %copy-start.4 = (f32[128]{0:T(128)S(1)}, f32[128]{0:T(128)}, u32[]{:S(2)}) copy-start(f32[128]{0:T(128)} %param.12) | copy-start | bytes 1540
  90.1 13.9 %collective-permute-start = (bf16[128,512]{1,0:T(8,128)(2,1)S(1)}, bf16[128,512]{1,0:T(8,128)(2,1)S(1)}, u32[]{:S(2)}, u32[]{:S(2)}) collective-permute-start(bf16[128,512]{1,0:T(8,128)(2,1)S(1)} %norm_back.1.refs_0_), channel_id=1, source_target_pairs={{0,16},{16,32},{32,48},{48,64},{64,80},{80,96},{96,112},{112,0},{1... | collective-permute-start | bytes 393224 | tf_op jit(solution)/shard_map/ppermute | solution.py:463
  91.9 12.3 %collective-permute-start.1 = (bf16[128,512]{1,0:T(8,128)(2,1)S(1)}, bf16[128,512]{1,0:T(8,128)(2,1)S(1)}, u32[]{:S(2)}, u32[]{:S(2)}) collective-permute-start(bf16[128,512]{1,0:T(8,128)(2,1)S(1)} %norm_back.1.refs_0_), channel_id=1, source_target_pairs={{0,32},{16,48},{32,64},{48,80},{64,96},{80,112},{96,0},{112,16},{1... | collective-permute-start | bytes 393224 | tf_op jit(solution)/shard_map/ppermute | solution.py:463
  91.9 17.9 %collective-permute-start.2 = (bf16[128,512]{1,0:T(8,128)(2,1)S(1)}, bf16[128,512]{1,0:T(8,128)(2,1)S(1)}, u32[]{:S(2)}, u32[]{:S(2)}) collective-permute-start(bf16[128,512]{1,0:T(8,128)(2,1)S(1)} %norm_back.1.refs_0_), channel_id=1, source_target_pairs={{0,48},{16,64},{32,80},{48,96},{64,112},{80,0},{96,16},{112,32},{1... | collective-permute-start | bytes 393224 | tf_op jit(solution)/shard_map/ppermute | solution.py:463
  96.4 13.4 %collective-permute-start.3 = (bf16[128,512]{1,0:T(8,128)(2,1)S(1)}, bf16[128,512]{1,0:T(8,128)(2,1)S(1)}, u32[]{:S(2)}, u32[]{:S(2)}) collective-permute-start(bf16[128,512]{1,0:T(8,128)(2,1)S(1)} %norm_back.1.refs_0_), channel_id=1, source_target_pairs={{0,64},{16,80},{32,96},{48,112},{64,0},{80,16},{96,32},{112,48},{1... | collective-permute-start | bytes 393224 | tf_op jit(solution)/shard_map/ppermute | solution.py:463
  97.6 12.2 %collective-permute-start.4 = (bf16[128,512]{1,0:T(8,128)(2,1)S(1)}, bf16[128,512]{1,0:T(8,128)(2,1)S(1)}, u32[]{:S(2)}, u32[]{:S(2)}) collective-permute-start(bf16[128,512]{1,0:T(8,128)(2,1)S(1)} %norm_back.1.refs_0_), channel_id=1, source_target_pairs={{0,80},{16,96},{32,112},{48,0},{64,16},{80,32},{96,48},{112,64},{1... | collective-permute-start | bytes 393224 | tf_op jit(solution)/shard_map/ppermute | solution.py:463
  104.0 6.5 %collective-permute-start.5 = (bf16[128,512]{1,0:T(8,128)(2,1)S(1)}, bf16[128,512]{1,0:T(8,128)(2,1)S(1)}, u32[]{:S(2)}, u32[]{:S(2)}) collective-permute-start(bf16[128,512]{1,0:T(8,128)(2,1)S(1)} %norm_back.1.refs_0_), channel_id=1, source_target_pairs={{0,96},{16,112},{32,0},{48,16},{64,32},{80,48},{96,64},{112,80},{1... | collective-permute-start | bytes 393224 | tf_op jit(solution)/shard_map/ppermute | solution.py:463
  104.2 6.3 %collective-permute-start.6 = (bf16[128,512]{1,0:T(8,128)(2,1)S(1)}, bf16[128,512]{1,0:T(8,128)(2,1)S(1)}, u32[]{:S(2)}, u32[]{:S(2)}) collective-permute-start(bf16[128,512]{1,0:T(8,128)(2,1)S(1)} %norm_back.1.refs_0_), channel_id=1, source_target_pairs={{0,112},{16,0},{32,16},{48,32},{64,48},{80,64},{96,80},{112,96},{1... | collective-permute-start | bytes 393224 | tf_op jit(solution)/shard_map/ppermute | solution.py:463
  113.2 16.6 %all-to-all-start.3 = ((bf16[8,120,512]{2,1,0:T(8,128)(2,1)}), bf16[8,120,512]{2,1,0:T(8,128)(2,1)S(1)}, u32[]{:S(2)}, u32[]{:S(2)}) async-start(bf16[8,120,512]{2,1,0:T(8,128)(2,1)} %bitcast.12), calls=%async_computation.3 | async-start | bytes 1966080 | tf_op jit(solution)/shard_map/all_to_all | solution.py:433
